TPU v7x, 768 devices: a whole 4x8x12 slice. The times are simulated.
768 devices in a mesh: depth: 24 (over x, z_lo), inslab: 32 (over y, z_hi, core).
Axes of the slice: x: 4, y: 8, z: 12 (z_hi: 2, z_lo: 6; z = z_hi * 6 + z_lo), core: 2. Of those that a mesh axis runs over, the one named last changes fastest.
Arguments:
- pressure: float32 [1536, 32, 1024], P(('depth', 'inslab')), may hold values from -6 to 6
- source: float32 [1536, 32, 1024], P(('depth', 'inslab')), may hold values from -4 to 4
- perm: float32 [1536, 32, 1024], P(('depth', 'inslab')), may hold values from 3e-07 to 3
- brinkman: float32 [1536], P(('depth', 'inslab')), may hold values from 0.5 to 4
- depth_source: int32 [1536, 2], P(('depth', 'inslab')), may hold values from -1 to 1, as said below
- sideways_neighbour_table: int32 [1536, 4], P(('depth', 'inslab')), may hold values from -1 to 65, as said below
- edge_blocks: int32 [768, 2, 2], P(('depth', 'inslab')), may hold values from 0 to 1, as said below
- restrict_take: int32 [1536], P(('depth', 'inslab')), may hold values from 0 to 63, as said below
Outputs:
- smoothed: float32 [1536, 32, 1024], P(('depth', 'inslab'))
- coarse_residual: float32 [1536, 16, 256], P(('depth', 'inslab'))
Inputs may be any that keep to these rules, and one draw needn't show every extreme that they name: `sideways_neighbour_table`: neighbour links are mutual: if block a names b in a direction, b names a in the opposite one. Devices of one depth index own disjoint strips of blocks of one slab; edge blocks of a peer are its rows facing the neighbour strip; a remote peer q is always the inslab index one below or one above the device's own. `depth_source`: links across depth are mutual and join blocks of the same inslab index on neighbouring depth indices. `edge_blocks`: each row lists distinct slots of the device. `restrict_take`: over the devices of one depth index, every fine block of the slab is named exactly once.
All inputs are finite; a program needn't handle non-finite values.
Results may differ from a plain program's by a relative error of at most 0.0003.
Values sent between devices are 32-bit elements; how exact they have to be, the bound alone decides.
A program may use at most 32 MiB of HBM per device.

v0:
```python
import jax
import jax.numpy as jnp
from jax import lax
from jax.sharding import PartitionSpec as P

OMEGA = 0.8


def extended(block, sides, width):
    for axis, dim in sides:
        count = lax.axis_size(axis)
        forward = [(i, i + 1) for i in range(count - 1)]
        backward = [(target, source) for source, target in forward]
        low = lax.ppermute(
            lax.slice_in_dim(block, block.shape[dim] - width, None, axis=dim), axis, forward
        )
        high = lax.ppermute(lax.slice_in_dim(block, 0, width, axis=dim), axis, backward)
        block = jnp.concatenate([low, block, high], axis=dim)
    return block


def from_behind(block, axis, distance):
    devices = range(lax.axis_size(axis))
    route = [(i - distance, i) for i in devices if i - distance in devices]
    return lax.ppermute(block, axis, route)


def block_faces(field):
    number, edge_len, plane_len = field.shape
    return [
        field[:, 0, :],
        field[:, -1, :],
        field[:, :, :edge_len].reshape(number, plane_len),
        field[:, :, plane_len - edge_len :].reshape(number, plane_len),
        field[:, :, 0::edge_len].reshape(number, plane_len),
        field[:, :, edge_len - 1 :: edge_len].reshape(number, plane_len),
    ]


def beside(field, ghosts):
    number, edge_len, plane_len = field.shape
    z_position = lax.broadcasted_iota(jnp.int32, (1, 1, plane_len), 2) % edge_len
    zero_cells = jnp.zeros((number, edge_len, 1), field.dtype)
    minus_x = jnp.concatenate([ghosts[0][:, None, :], field[:, :-1, :]], axis=1)
    plus_x = jnp.concatenate([field[:, 1:, :], ghosts[1][:, None, :]], axis=1)
    minus_y = jnp.concatenate(
        [ghosts[2].reshape(number, edge_len, edge_len), field[:, :, : plane_len - edge_len]], axis=2
    )
    plus_y = jnp.concatenate(
        [field[:, :, edge_len:], ghosts[3].reshape(number, edge_len, edge_len)], axis=2
    )
    minus_z = jnp.where(
        z_position == 0,
        jnp.repeat(ghosts[4].reshape(number, edge_len, edge_len), edge_len, axis=2),
        jnp.concatenate([zero_cells, field[:, :, :-1]], axis=2),
    )
    plus_z = jnp.where(
        z_position == edge_len - 1,
        jnp.repeat(ghosts[5].reshape(number, edge_len, edge_len), edge_len, axis=2),
        jnp.concatenate([field[:, :, 1:], zero_cells], axis=2),
    )
    return [minus_x, plus_x, minus_y, plus_y, minus_z, plus_z]


def coefficients(perm, kghosts, brinkman):
    face_weights = [
        2.0 * perm * neighbour / (perm + neighbour) for neighbour in beside(perm, kghosts)
    ]
    diagonal = (
        brinkman[:, None, None]
        + face_weights[0]
        + face_weights[1]
        + face_weights[2]
        + face_weights[3]
        + face_weights[4]
        + face_weights[5]
    )
    return (face_weights, diagonal)


def operate(field, ghosts, face_weights, diagonal):
    neighbours = beside(field, ghosts)
    flux = face_weights[0] * neighbours[0]
    for direction in range(1, 6):
        flux = flux + face_weights[direction] * neighbours[direction]
    return diagonal * field - flux


def restrict(residual):
    number, edge_len, plane_len = residual.shape
    half_len = edge_len // 2
    paired = residual[:, 0::2, :] + residual[:, 1::2, :]
    row_index = lax.broadcasted_iota(jnp.int32, (plane_len, half_len * half_len), 0)
    column = lax.broadcasted_iota(jnp.int32, (plane_len, half_len * half_len), 1)
    target = row_index // edge_len // 2 * half_len + row_index % edge_len // 2
    pooling = (target == column).astype(jnp.float32)
    return 0.125 * jnp.einsum("bxp,pq->bxq", paired, pooling, precision=lax.Precision.HIGHEST)


def select_rows(pool, requested_blocks):
    gathered_rows = jnp.take(pool, jnp.maximum(requested_blocks, 0), axis=1)
    return jnp.where((requested_blocks >= 0)[None, :, None], gathered_rows, 0.0)


def body(
    pressure,
    source,
    perm,
    brinkman,
    depth_source,
    sideways_neighbour_table,
    edge_blocks,
    restrict_take,
):
    block_count = pressure.shape[0]
    edge_count = edge_blocks.shape[2]
    my_index = lax.axis_index("inslab")

    def relabel_blocks(neighbour_value):
        remote = neighbour_value - block_count
        upper_side = (remote // edge_count > my_index).astype(jnp.int32)
        return jnp.where(
            neighbour_value >= block_count,
            block_count + upper_side * edge_count + remote % edge_count,
            neighbour_value,
        )

    def ghost_faces(fields):
        field_count = len(fields)
        all_faces = [block_faces(member) for member in fields]
        own_faces = [
            jnp.stack([listed[direction] for listed in all_faces]) for direction in range(6)
        ]
        layers = extended(jnp.stack([own_faces[0], own_faces[1]]), (("depth", 0),), 1)
        low_edge = jnp.take(own_faces[2], edge_blocks[0, 0], axis=1)
        high_edge = jnp.take(own_faces[3], edge_blocks[0, 1], axis=1)
        both_edges = jnp.stack([low_edge, high_edge], axis=1)
        from_lower = from_behind(both_edges, "inslab", 1)
        from_upper = from_behind(both_edges, "inslab", -1)
        for_minus = jnp.concatenate([from_lower[:, 1], from_upper[:, 1]], axis=1)
        for_plus = jnp.concatenate([from_lower[:, 0], from_upper[:, 0]], axis=1)
        lower_direction_index = relabel_blocks(sideways_neighbour_table[:, 0])
        upper_direction_index = relabel_blocks(sideways_neighbour_table[:, 1])
        ghost_list = [
            select_rows(layers[0], depth_source[:, 0]),
            select_rows(layers[3], depth_source[:, 1]),
            select_rows(jnp.concatenate([own_faces[3], for_minus], axis=1), lower_direction_index),
            select_rows(jnp.concatenate([own_faces[2], for_plus], axis=1), upper_direction_index),
            select_rows(own_faces[5], sideways_neighbour_table[:, 2]),
            select_rows(own_faces[4], sideways_neighbour_table[:, 3]),
        ]
        return [[ghost[member] for ghost in ghost_list] for member in range(field_count)]

    peer_ghost_blocks, kghosts = ghost_faces([pressure, perm])
    stored = coefficients(perm, kghosts, brinkman)
    pressure_now = pressure
    for iteration in range(2):
        face_weights, diagonal = stored
        applied = operate(pressure_now, peer_ghost_blocks, face_weights, diagonal)
        pressure_now = pressure_now + OMEGA * (source - applied) / diagonal
        peer_ghost_blocks = ghost_faces([pressure_now])[0]
    face_weights, diagonal = stored
    residual = source - operate(pressure_now, peer_ghost_blocks, face_weights, diagonal)
    pieces = restrict(residual)
    piece = lax.all_gather(pieces, "inslab", axis=0, tiled=True)
    inside = (restrict_take >= 0) & (restrict_take < piece.shape[0])
    taken = jnp.take(piece, jnp.clip(restrict_take, 0, piece.shape[0] - 1), axis=0)
    coarse = jnp.where(inside[:, None, None], taken, jnp.zeros_like(pieces))
    return (pressure_now, coarse)


def solution(mesh):
    return jax.shard_map(
        body,
        mesh=mesh,
        in_specs=(
            P(("depth", "inslab"), None, None),
            P(("depth", "inslab"), None, None),
            P(("depth", "inslab"), None, None),
            P(("depth", "inslab")),
            P(("depth", "inslab"), None),
            P(("depth", "inslab"), None),
            P(("depth", "inslab"), None, None),
            P(("depth", "inslab")),
        ),
        out_specs=(P(("depth", "inslab"), None, None), P(("depth", "inslab"), None, None)),
        check_vma=False,
    )
```

profile of v0, /device:TPU:7, one launch (start us, length us, event | category | flops | bytes accessed | tf_op | source)
XLA Modules:
  0.0 259.3 jit_solution(1630123220450465986)
XLA Ops:
  8.9 0.9 fusion.100
  11.4 15.4 %collective-permute-start.2 = (f32[2,2,2,1024]{3,0,2,1:T(2,128)S(1)}, f32[2,2,2,1024]{3,0,2,1:T(2,128)S(1)}, u32[]{:S(2)}, u32[]{:S(2)}) collective-permute-start(f32[2,2,2,1024]{3,0,2,1:T(2,128)S(1)} %pad_maximum_fusion.6), channel_id=1, source_target_pairs={{0,1},{1,2},{2,3},{3,4},{4,5},{5,6},{6,7},{7,8},{8,9},{9,10},{10,1... | collective-permute-start | bytes 98312 | tf_op jit(solution)/shard_map/ppermute | solution.py:25
  26.9 1.9 collective-permute-start.3
  28.9 3.1 %collective-permute-start = (f32[1,2,2,1024]{3,1,2,0:T(2,128)S(1)}, f32[1,2,2,1024]{3,1,2,0:T(2,128)S(1)}, u32[]{:S(2)}, u32[]{:S(2)}) collective-permute-start(f32[1,2,2,1024]{3,1,2,0:T(2,128)S(1)} %maximum_bitcast_fusion.4), channel_id=1, source_target_pairs={{0,32},{32,64},{64,96},{96,128},{128,160},{160,192},{192,224},{224... | collective-permute-start | bytes 49160 | tf_op jit(solution)/shard_map/ppermute | solution.py:14
  32.0 7.9 %collective-permute-start.1 = (f32[1,2,2,1024]{3,1,2,0:T(2,128)S(1)}, f32[1,2,2,1024]{3,1,2,0:T(2,128)S(1)}, u32[]{:S(2)}, u32[]{:S(2)}) collective-permute-start(f32[1,2,2,1024]{3,1,2,0:T(2,128)S(1)} %maximum_bitcast_fusion.5), channel_id=1, source_target_pairs={{32,0},{64,32},{96,64},{128,96},{160,128},{192,160},{224,192},{256... | collective-permute-start | bytes 49160 | tf_op jit(solution)/shard_map/ppermute | solution.py:17
  42.6 1.0 fusion.94
  43.7 1.2 fusion.95
  44.9 1.1 fusion.96
  50.1 1.2 reshape.159
  51.7 1.2 reshape.160
  53.3 1.2 reshape.161
  55.0 1.2 reshape.162
  60.1 2.7 %fusion.34 = (f32[2,32,1024]{2,1,0:T(8,128)S(1)}, f32[2,32,1024]{2,1,0:T(8,128)S(1)}, f32[2,32,1024]{2,1,0:T(8,128)S(1)}, f32[2,32,1024]{2,1,0:T(8,128)S(1)}, f3...) fusion(f32[2,32,1024]{2,1,0:T(8,128)S(1)} %copy-done.1, ...), kind=kLoop, calls=%fused_computation.78 | loop fusion | flops 3538944 | bytes 6816776 | tf_op jit(solution)/shard_map/add | solution.py:160
  64.3 10.5 %collective-permute-start.6 = (f32[1,2,2,1024]{3,2,1,0:T(2,128)S(1)}, f32[1,2,2,1024]{3,2,1,0:T(2,128)S(1)}, u32[]{:S(2)}, u32[]{:S(2)}) collective-permute-start(f32[1,2,2,1024]{3,2,1,0:T(2,128)S(1)} %pad_maximum_fusion.11), channel_id=1, source_target_pairs={{0,1},{1,2},{2,3},{3,4},{4,5},{5,6},{6,7},{7,8},{8,9},{9,10},{10,1... | collective-permute-start | bytes 49160 | tf_op jit(solution)/shard_map/ppermute | solution.py:25
  74.9 1.9 collective-permute-start.7
  77.5 0.9 fusion.90
  78.4 0.9 fusion.91
  81.5 1.9 collective-permute-start.4
  84.1 1.2 reshape.163
  85.7 1.2 reshape.164
  86.9 9.1 %collective-permute-start.5 = (f32[1,1,2,1024]{3,0,2,1:T(1,128)S(1)}, f32[1,1,2,1024]{3,0,2,1:T(1,128)S(1)}, u32[]{:S(2)}, u32[]{:S(2)}) collective-permute-start(f32[1,1,2,1024]{3,0,2,1:T(1,128)S(1)} %get-tuple-element.65), channel_id=1, source_target_pairs={{32,0},{64,32},{96,64},{128,96},{160,128},{192,160},{224,192},{256... | collective-permute-start | bytes 24584 | tf_op jit(solution)/shard_map/ppermute | solution.py:17
  99.1 1.8 fusion.44
  102.5 11.1 %collective-permute-start.10 = (f32[1,2,2,1024]{3,2,1,0:T(2,128)S(1)}, f32[1,2,2,1024]{3,2,1,0:T(2,128)S(1)}, u32[]{:S(2)}, u32[]{:S(2)}) collective-permute-start(f32[1,2,2,1024]{3,2,1,0:T(2,128)S(1)} %pad_maximum_fusion.12), channel_id=1, source_target_pairs={{0,1},{1,2},{2,3},{3,4},{4,5},{5,6},{6,7},{7,8},{8,9},{9,10},{10,1... | collective-permute-start | bytes 49160 | tf_op jit(solution)/shard_map/ppermute | solution.py:25
  113.6 2.1 collective-permute-start.11
  116.4 0.9 fusion.86
  121.0 1.9 collective-permute-start.8
  124.5 1.2 reshape.166
  125.7 9.1 %collective-permute-start.9 = (f32[1,1,2,1024]{3,0,2,1:T(1,128)S(1)}, f32[1,1,2,1024]{3,0,2,1:T(1,128)S(1)}, u32[]{:S(2)}, u32[]{:S(2)}) collective-permute-start(f32[1,1,2,1024]{3,0,2,1:T(1,128)S(1)} %get-tuple-element.55), channel_id=1, source_target_pairs={{32,0},{64,32},{96,64},{128,96},{160,128},{192,160},{224,192},{256... | collective-permute-start | bytes 24584 | tf_op jit(solution)/shard_map/ppermute | solution.py:17
  139.1 1.7 fusion.51
  141.6 1.8 convolution_multiply_fusion
  144.1 105.9 %all-gather.2.cloned.1.call-done = f32[64,16,256]{2,1,0:T(8,128)} async-done(((f32[2,16,256]{2,1,0:T(8,128)}), f32[64,16,256]{2,1,0:T(8,128)}) %all-gather.2.cloned.1.call-update) | async-done | bytes 1048592 | tf_op jit(solution)/shard_map/all_gather | solution.py:165
  250.0 1.8 gather_fusion
  (253 shorter events, 37.3 us)
Async XLA Ops:
  7.2 242.9 %all-gather.2.cloned.1.call-start = ((), (), s32[]{:S(2)}) async-start(), calls=%async_computation | async-start | bytes 1081344 | tf_op jit(solution)/shard_map/all_gather | solution.py:165
  8.9 19.9 %copy-start.1 = (f32[2,32,1024]{2,1,0:T(8,128)S(1)}, f32[2,32,1024]{2,1,0:T(8,128)}, u32[]{:S(2)}) copy-start(f32[2,32,1024]{2,1,0:T(8,128)} %param.16) | copy-start | bytes 786436
  8.9 19.9 %copy-start.2 = (f32[2,32,1024]{2,1,0:T(8,128)S(1)}, f32[2,32,1024]{2,1,0:T(8,128)}, u32[]{:S(2)}) copy-start(f32[2,32,1024]{2,1,0:T(8,128)} %param.18) | copy-start | bytes 786436
  11.4 46.1 %collective-permute-start.2 = (f32[2,2,2,1024]{3,0,2,1:T(2,128)S(1)}, f32[2,2,2,1024]{3,0,2,1:T(2,128)S(1)}, u32[]{:S(2)}, u32[]{:S(2)}) collective-permute-start(f32[2,2,2,1024]{3,0,2,1:T(2,128)S(1)} %pad_maximum_fusion.6), channel_id=1, source_target_pairs={{0,1},{1,2},{2,3},{3,4},{4,5},{5,6},{6,7},{7,8},{8,9},{9,10},{10,1... | collective-permute-start | bytes 98312 | tf_op jit(solution)/shard_map/ppermute | solution.py:25
  26.9 30.7 %collective-permute-start.3 = (f32[2,2,2,1024]{3,0,2,1:T(2,128)S(1)}, f32[2,2,2,1024]{3,0,2,1:T(2,128)S(1)}, u32[]{:S(2)}, u32[]{:S(2)}) collective-permute-start(f32[2,2,2,1024]{3,0,2,1:T(2,128)S(1)} %pad_maximum_fusion.6), channel_id=1, source_target_pairs={{1,0},{2,1},{3,2},{4,3},{5,4},{6,5},{7,6},{8,7},{9,8},{10,9},{11,1... | collective-permute-start | bytes 98312 | tf_op jit(solution)/shard_map/ppermute | solution.py:25
  28.9 27.3 %collective-permute-start = (f32[1,2,2,1024]{3,1,2,0:T(2,128)S(1)}, f32[1,2,2,1024]{3,1,2,0:T(2,128)S(1)}, u32[]{:S(2)}, u32[]{:S(2)}) collective-permute-start(f32[1,2,2,1024]{3,1,2,0:T(2,128)S(1)} %maximum_bitcast_fusion.4), channel_id=1, source_target_pairs={{0,32},{32,64},{64,96},{96,128},{128,160},{160,192},{192,224},{224... | collective-permute-start | bytes 49160 | tf_op jit(solution)/shard_map/ppermute | solution.py:14
  32.0 7.9 %copy-start.10 = (s32[2,4]{1,0:T(2,128)S(1)}, s32[2,4]{1,0:T(2,128)}, u32[]{:S(2)}) copy-start(s32[2,4]{1,0:T(2,128)} %param.21) | copy-start | bytes 100
  32.0 24.8 %collective-permute-start.1 = (f32[1,2,2,1024]{3,1,2,0:T(2,128)S(1)}, f32[1,2,2,1024]{3,1,2,0:T(2,128)S(1)}, u32[]{:S(2)}, u32[]{:S(2)}) collective-permute-start(f32[1,2,2,1024]{3,1,2,0:T(2,128)S(1)} %maximum_bitcast_fusion.5), channel_id=1, source_target_pairs={{32,0},{64,32},{96,64},{128,96},{160,128},{192,160},{224,192},{256... | collective-permute-start | bytes 49160 | tf_op jit(solution)/shard_map/ppermute | solution.py:17
  40.2 58.7 %copy-start.16 = (pred[2]{0:T(512)(128)(4,1)}, pred[2]{0:T(512)(128)(4,1)S(1)}, u32[]{:S(2)}) copy-start(pred[2]{0:T(512)(128)(4,1)S(1)} %broadcast_compare_fusion.1) | copy-start | bytes 10
  40.2 57.8 %copy-start.18 = (pred[2]{0:T(512)(128)(4,1)}, pred[2]{0:T(512)(128)(4,1)S(1)}, u32[]{:S(2)}) copy-start(pred[2]{0:T(512)(128)(4,1)S(1)} %broadcast_compare_fusion) | copy-start | bytes 10
  42.4 54.2 %copy-start.22 = (pred[2]{0:T(512)(128)(4,1)}, pred[2]{0:T(512)(128)(4,1)S(1)}, u32[]{:S(2)}) copy-start(pred[2]{0:T(512)(128)(4,1)S(1)} %compare_and_fusion.5) | copy-start | bytes 10
  42.6 54.7 %copy-start.20 = (pred[2]{0:T(512)(128)(4,1)}, pred[2]{0:T(512)(128)(4,1)S(1)}, u32[]{:S(2)}) copy-start(pred[2]{0:T(512)(128)(4,1)S(1)} %compare_and_fusion.4) | copy-start | bytes 10
  47.2 51.1 %copy-start.12 = (s32[1024]{0:T(1024)}, s32[1024]{0:T(1024)S(1)}, u32[]{:S(2)}) copy-start(s32[1024]{0:T(1024)S(1)} %pad_clamp_fusion.4) | copy-start | bytes 12292
  47.2 50.3 %copy-start.13 = (s32[1024]{0:T(1024)}, s32[1024]{0:T(1024)S(1)}, u32[]{:S(2)}) copy-start(s32[1024]{0:T(1024)S(1)} %pad_clamp_fusion.3) | copy-start | bytes 12292
  49.1 47.0 %copy-start.15 = (s32[1024]{0:T(1024)}, s32[1024]{0:T(1024)S(1)}, u32[]{:S(2)}) copy-start(s32[1024]{0:T(1024)S(1)} %pad_clamp_fusion.8) | copy-start | bytes 12292
  49.1 47.7 %copy-start.14 = (s32[1024]{0:T(1024)}, s32[1024]{0:T(1024)S(1)}, u32[]{:S(2)}) copy-start(s32[1024]{0:T(1024)S(1)} %pad_clamp_fusion.7) | copy-start | bytes 12292
  57.5 2.0 copy-start.9
  64.3 33.1 %collective-permute-start.6 = (f32[1,2,2,1024]{3,2,1,0:T(2,128)S(1)}, f32[1,2,2,1024]{3,2,1,0:T(2,128)S(1)}, u32[]{:S(2)}, u32[]{:S(2)}) collective-permute-start(f32[1,2,2,1024]{3,2,1,0:T(2,128)S(1)} %pad_maximum_fusion.11), channel_id=1, source_target_pairs={{0,1},{1,2},{2,3},{3,4},{4,5},{5,6},{6,7},{7,8},{8,9},{9,10},{10,1... | collective-permute-start | bytes 49160 | tf_op jit(solution)/shard_map/ppermute | solution.py:25
  74.9 22.6 %collective-permute-start.7 = (f32[1,2,2,1024]{3,2,1,0:T(2,128)S(1)}, f32[1,2,2,1024]{3,2,1,0:T(2,128)S(1)}, u32[]{:S(2)}, u32[]{:S(2)}) collective-permute-start(f32[1,2,2,1024]{3,2,1,0:T(2,128)S(1)} %pad_maximum_fusion.11), channel_id=1, source_target_pairs={{1,0},{2,1},{3,2},{4,3},{5,4},{6,5},{7,6},{8,7},{9,8},{10,9},{11,1... | collective-permute-start | bytes 49160 | tf_op jit(solution)/shard_map/ppermute | solution.py:25
  81.5 14.5 %collective-permute-start.4 = (f32[1,1,2,1024]{3,0,2,1:T(1,128)S(1)}, f32[1,1,2,1024]{3,0,2,1:T(1,128)S(1)}, u32[]{:S(2)}, u32[]{:S(2)}) collective-permute-start(f32[1,1,2,1024]{3,0,2,1:T(1,128)S(1)} %get-tuple-element.66), channel_id=1, source_target_pairs={{0,32},{32,64},{64,96},{96,128},{128,160},{160,192},{192,224},{224... | collective-permute-start | bytes 24584 | tf_op jit(solution)/shard_map/ppermute | solution.py:14
  86.9 9.8 %collective-permute-start.5 = (f32[1,1,2,1024]{3,0,2,1:T(1,128)S(1)}, f32[1,1,2,1024]{3,0,2,1:T(1,128)S(1)}, u32[]{:S(2)}, u32[]{:S(2)}) collective-permute-start(f32[1,1,2,1024]{3,0,2,1:T(1,128)S(1)} %get-tuple-element.65), channel_id=1, source_target_pairs={{32,0},{64,32},{96,64},{128,96},{160,128},{192,160},{224,192},{256... | collective-permute-start | bytes 24584 | tf_op jit(solution)/shard_map/ppermute | solution.py:17
  96.8 2.3 copy-start.6
  100.9 37.5 %copy-start = (f32[2,32,1024]{2,1,0:T(8,128)}, f32[2,32,1024]{2,1,0:T(8,128)S(1)}, u32[]{:S(2)}) copy-start(f32[2,32,1024]{2,1,0:T(8,128)S(1)} %fusion.44) | copy-start | bytes 786436
  102.5 34.1 %collective-permute-start.10 = (f32[1,2,2,1024]{3,2,1,0:T(2,128)S(1)}, f32[1,2,2,1024]{3,2,1,0:T(2,128)S(1)}, u32[]{:S(2)}, u32[]{:S(2)}) collective-permute-start(f32[1,2,2,1024]{3,2,1,0:T(2,128)S(1)} %pad_maximum_fusion.12), channel_id=1, source_target_pairs={{0,1},{1,2},{2,3},{3,4},{4,5},{5,6},{6,7},{7,8},{8,9},{9,10},{10,1... | collective-permute-start | bytes 49160 | tf_op jit(solution)/shard_map/ppermute | solution.py:25
  113.6 23.0 %collective-permute-start.11 = (f32[1,2,2,1024]{3,2,1,0:T(2,128)S(1)}, f32[1,2,2,1024]{3,2,1,0:T(2,128)S(1)}, u32[]{:S(2)}, u32[]{:S(2)}) collective-permute-start(f32[1,2,2,1024]{3,2,1,0:T(2,128)S(1)} %pad_maximum_fusion.12), channel_id=1, source_target_pairs={{1,0},{2,1},{3,2},{4,3},{5,4},{6,5},{7,6},{8,7},{9,8},{10,9},{11,1... | collective-permute-start | bytes 49160 | tf_op jit(solution)/shard_map/ppermute | solution.py:25
  121.0 13.8 %collective-permute-start.8 = (f32[1,1,2,1024]{3,0,2,1:T(1,128)}, f32[1,1,2,1024]{3,0,2,1:T(1,128)S(1)}, u32[]{:S(2)}, u32[]{:S(2)}) collective-permute-start(f32[1,1,2,1024]{3,0,2,1:T(1,128)} %get-tuple-element.56), channel_id=1, source_target_pairs={{0,32},{32,64},{64,96},{96,128},{128,160},{160,192},{192,224},{224... | collective-permute-start | bytes 24584 | tf_op jit(solution)/shard_map/ppermute | solution.py:14
  124.5 12.0 %copy-start.21 = (pred[2]{0:T(512)(128)(4,1)S(1)}, pred[2]{0:T(512)(128)(4,1)}, u32[]{:S(2)}) copy-start(pred[2]{0:T(512)(128)(4,1)} %copy-done.20) | copy-start | bytes 10
  125.7 9.9 %collective-permute-start.9 = (f32[1,1,2,1024]{3,0,2,1:T(1,128)S(1)}, f32[1,1,2,1024]{3,0,2,1:T(1,128)S(1)}, u32[]{:S(2)}, u32[]{:S(2)}) collective-permute-start(f32[1,1,2,1024]{3,0,2,1:T(1,128)S(1)} %get-tuple-element.55), channel_id=1, source_target_pairs={{32,0},{64,32},{96,64},{128,96},{160,128},{192,160},{224,192},{256... | collective-permute-start | bytes 24584 | tf_op jit(solution)/shard_map/ppermute | solution.py:17
  134.8 2.5 copy-start.19
  134.8 3.4 %copy-start.17 = (pred[2]{0:T(512)(128)(4,1)S(1)}, pred[2]{0:T(512)(128)(4,1)}, u32[]{:S(2)}) copy-start(pred[2]{0:T(512)(128)(4,1)} %copy-done.16) | copy-start | bytes 10
  135.6 2.8 %copy-start.4 = (f32[2,32,1024]{2,1,0:T(8,128)S(1)}, f32[2,32,1024]{2,1,0:T(8,128)}, u32[]{:S(2)}) copy-start(f32[2,32,1024]{2,1,0:T(8,128)} %reshape.166) | copy-start | bytes 786436
  135.6 2.8 %copy-start.7 = (f32[2,32,1023]{2,1,0:T(8,128)S(1)}, f32[2,32,1023]{2,1,0:T(8,128)}, u32[]{:S(2)}) copy-start(f32[2,32,1023]{2,1,0:T(8,128)} %get-tuple-element.47) | copy-start | bytes 785668
  (14 other events, 12.9 us)
Sparse Core Ops, SparseCore 0:
  143.6 106.3 all-gather.1
where the time goes:
time: 261 us; the launch traced here: 259 us
  waiting for transfers between devices  106 us (41%)
  starting transfers between devices  75.9 us (29%)
  local copies, waits for them, and re-layouts  47.8 us (18%)
  between operations  15.1 us (6%)
  other arithmetic  12.7 us (5%)
    all_gather x1, waiting for transfers between devices, body(): piece = lax.all_gather(pieces, 'inslab', axis=0, tiled=True)  106 us
    ppermute x6, starting transfers between devices, from_behind(): return lax.ppermute(block, axis, route)  43 us
    ppermute x3, starting transfers between devices, extended(): lax.ppermute(lax.slice_in_dim(block, 0, width, axis=dim), axis, backward)  26 us
    gather x18, local copies, waits for them, and re-layouts, select_rows(): gathered_rows = jnp.take(pool, jnp.maximum(requested_blocks, 0), axis=1)  10.8 us
    ppermute x3, starting transfers between devices, extended(): lax.ppermute(lax.slice_in_dim(block, block.shape[dim] - width, None, axis...  6.94 us
  transfers between devices with their start and end apart: 13, of which 2 were waited for; matrix products, arithmetic and copies ran while one was open for 14% of the time, Pallas kernels for 0%

commit v1 on v0

v1 whole, which is shorter than its diff:
```python
import jax
import jax.numpy as jnp
from jax import lax
from jax.experimental import pallas as pl
from jax.experimental.pallas import tpu as pltpu
from jax.sharding import PartitionSpec as P

OMEGA = 0.8
MESH = pl.DeviceIdType.MESH
F32 = jnp.float32
CHUNKS, SUB, LANES = 4, 8, 1024


def kernel(
    p_hbm, s_hbm, k_hbm, brink, ds, snt, eb, take,
    out_hbm, coarse_hbm,
    u0, src, perm, u1, u2, g, dg, inv, wxm, wxp, wym, wyp, wzm, wzp,
    wxlo, wxhi, wylo, wyhi, res, pool,
    xs1, xs2, xs3, xr1, xr2, xr3, ys1, ys2, ys3, yr1, yr2, yr3,
    wants, gathered, sib_out, sib_in, zp_out, zp_in, coarse,
    in_sem, out_sem, hs_sem, hr_sem, ws_sem, wr_sem, gs_sem, gr_sem, es_sem, er_sem,
):
    depth = lax.axis_index("depth")
    me = lax.axis_index("inslab")
    n_depth = lax.axis_size("depth")
    n_in = lax.axis_size("inslab")
    n_y = n_in // 4
    my_y = me // 4
    zh = (me // 2) % 2
    core = me % 2

    def at(y, z, c):
        return (depth, (y * 2 + z) * 2 + c)

    d_low = (lax.rem(depth + n_depth - 1, n_depth), me)
    d_high = (lax.rem(depth + 1, n_depth), me)
    i_low = (depth, lax.rem(me + n_in - 1, n_in))
    i_high = (depth, lax.rem(me + 1, n_in))
    sib = at(my_y, zh, 1 - core)
    zpar = at(my_y, 1 - zh, core)
    zdia = at(my_y, 1 - zh, 1 - core)
    y_peers = [at(lax.rem(my_y + o, n_y), zh, core) for o in range(1, n_y)]

    loads = [
        pltpu.make_async_copy(h, v, in_sem.at[i])
        for i, (h, v) in enumerate([(k_hbm, perm), (p_hbm, u0), (s_hbm, src)])
    ]
    for load in loads:
        load.start()

    barrier = pltpu.get_barrier_semaphore()
    partners = [d_low, d_high, i_low, i_high, sib, zpar, zdia] + y_peers
    for partner in partners:
        pl.semaphore_signal(barrier, inc=1, device_id=partner, device_id_type=MESH)

    lane128 = lax.broadcasted_iota(jnp.int32, (CHUNKS, SUB, 128), 2)
    row = lax.broadcasted_iota(jnp.int32, (SUB, LANES), 0)
    lane = lax.broadcasted_iota(jnp.int32, (SUB, LANES), 1)
    zpos = lane % 32

    def remote(a, b, s, r, device):
        copy = pltpu.make_async_remote_copy(
            src_ref=a, dst_ref=b, send_sem=s, recv_sem=r, device_id=device, device_id_type=MESH
        )
        copy.start()
        return copy

    wrow = lax.broadcasted_iota(jnp.int32, (SUB, 128), 0)
    wants[0] = jnp.where(wrow < 4, take[0], take[1])

    def faces_minus(limit_low):
        found = False
        for a in range(2):
            w = snt[a, 0]
            remote_w = w >= 2
            low = w - 2 < 2 * me
            hit = remote_w & (low if limit_low else jnp.logical_not(low))
            found = hit if a == 0 else found | hit
        return found

    low_is_minus = faces_minus(True)
    high_is_minus = faces_minus(False)

    def y_faces(field):
        low = [field[a, :, :, 0:128] for a in range(2)]
        high = [pltpu.roll(field[a, :, :, LANES - 128 : LANES], 32, 2) for a in range(2)]
        return low, high

    def pair_for(faces, minus):
        low, high = faces
        cols = []
        for c in range(2):
            from_low = jnp.where(eb[0, 0, c] == 1, low[1], low[0])
            from_high = jnp.where(eb[0, 1, c] == 1, high[1], high[0])
            cols.append(jnp.where(minus, from_low, from_high))
        return jnp.where(lane128 < 32, cols[0], pltpu.roll(cols[1], 32, 2))

    def fold(pair):
        half = CHUNKS // 2
        return jnp.where(
            lane128[:half] < 64, pair[:half], pltpu.roll(pair[half:], 64, 2)
        )

    def unfold(packed):
        return jnp.concatenate([packed, pltpu.roll(packed, 64, 2)], axis=0)

    def x_faces(field, low):
        if low:
            return [field[a, 0, 0:1, :] for a in range(2)]
        return [field[a, CHUNKS - 1, SUB - 1 : SUB, :] for a in range(2)]

    def send_round(number, xs, ys, xr, yr):
        base = 4 * number
        return [
            remote(ys.at[0], yr.at[1], hs_sem.at[base], hr_sem.at[base], i_low),
            remote(ys.at[1], yr.at[0], hs_sem.at[base + 1], hr_sem.at[base + 1], i_high),
            remote(xs.at[0], xr.at[1], hs_sem.at[base + 2], hr_sem.at[base + 2], d_low),
            remote(xs.at[1], xr.at[0], hs_sem.at[base + 3], hr_sem.at[base + 3], d_high),
        ]

    def fill_x(xs, first, field):
        for side in range(2):
            for a, face in enumerate(x_faces(field, side == 0)):
                xs[side, first + a : first + a + 1, :] = face

    loads[0].wait()
    loads[1].wait()
    fill_x(xs1, 0, u0)
    fill_x(xs1, 2, perm)
    for side, minus in enumerate((low_is_minus, high_is_minus)):
        pp = pair_for(y_faces(u0), minus)
        kk = pair_for(y_faces(perm), minus)
        ys1[side] = jnp.where(lane128 < 64, pp, pltpu.roll(kk, 64, 2))
    pl.semaphore_wait(barrier, len(partners))
    sent = send_round(0, xs1, ys1, xr1, yr1)
    want_copies = [
        remote(wants.at[0], wants.at[1 + j], ws_sem.at[j], wr_sem.at[j], device)
        for j, device in enumerate((sib, zpar, zdia))
    ]

    def zslot(a, direction):
        return jnp.maximum(snt[a, 2 + direction], 0)

    def beside(field, a, k):
        u = field[a, k]
        before = field[a, jnp.maximum(k - 1, 0), SUB - 1 : SUB, :]
        after = field[a, jnp.minimum(k + 1, CHUNKS - 1), 0:1, :]
        um = jnp.where(row == 0, before, pltpu.roll(u, 1, 0))
        up = jnp.where(row == SUB - 1, after, pltpu.roll(u, SUB - 1, 0))
        ym = pltpu.roll(u, 32, 1)
        yp = pltpu.roll(u, LANES - 32, 1)
        nm = field[zslot(a, 0), k]
        np_ = field[zslot(a, 1), k]
        zm = jnp.where(zpos == 0, pltpu.roll(nm, LANES - 31, 1), pltpu.roll(u, 1, 1))
        zp = jnp.where(zpos == 31, pltpu.roll(np_, 31, 1), pltpu.roll(u, LANES - 1, 1))
        return u, (um, up, ym, yp, zm, zp)

    def weights(k, _):
        for a in range(2):
            kk, nbs = beside(perm, a, k)
            has_zm = snt[a, 2] >= 0
            has_zp = snt[a, 3] >= 0
            keep = (
                jnp.logical_not((row == 0) & (k == 0)),
                jnp.logical_not((row == SUB - 1) & (k == CHUNKS - 1)),
                lane >= 32,
                lane < LANES - 32,
                jnp.logical_or(zpos != 0, has_zm),
                jnp.logical_or(zpos != 31, has_zp),
            )
            total = jnp.full((SUB, LANES), brink[a], F32)
            for store, nb, mask in zip((wxm, wxp, wym, wyp, wzm, wzp), nbs, keep):
                w = jnp.where(mask, 2.0 * kk * nb / (kk + nb), 0.0)
                store[a, k] = w
                total = total + w
            dg[a, k] = total
        return 0

    lax.fori_loop(0, CHUNKS, weights, 0)
    loads[2].wait()

    def neighbour_sum(field):
        def step(k, _):
            for a in range(2):
                _, nbs = beside(field, a, k)
                total = src[a, k]
                for store, nb in zip((wxm, wxp, wym, wyp, wzm, wzp), nbs):
                    total = total + store[a, k] * nb
                g[a, k] = total
            return 0

        lax.fori_loop(0, CHUNKS, step, 0)

    neighbour_sum(u0)

    prow = lax.broadcasted_iota(jnp.int32, (512, 128), 0)
    pcol = lax.broadcasted_iota(jnp.int32, (512, 128), 1)
    pool[...] = ((prow // 64) * 16 + (prow % 32) // 2 == pcol).astype(F32)

    def x_ghost(message, a, direction, first):
        slot = ds[a, direction]
        zero = jnp.zeros((1, LANES), F32)
        return jnp.where(
            slot == 0,
            message[first : first + 1, :],
            jnp.where(slot == 1, message[first + 1 : first + 2, :], zero),
        )

    def y_ghost(faces, pairs, a, direction):
        w = snt[a, direction]
        c1 = w % 2 == 1
        from_low = w - 2 < 2 * me
        low_pair, high_pair = pairs
        pair = jnp.where(from_low, low_pair, high_pair)
        far = jnp.where(c1, pltpu.roll(pair, 96, 2), pair)
        near = jnp.where(w == 1, faces[1], faces[0])
        found = jnp.where(w >= 2, far, near)
        return jnp.where((lane128 < 32) & (w >= 0), found, 0.0)

    def harmonic(a, b):
        return 2.0 * a * b / (a + b)

    for copy in sent:
        copy.wait_recv()

    k_low, k_high = y_faces(perm)
    u_low, u_high = y_faces(u0)
    k_pairs = [pltpu.roll(yr1[i], 64, 2) for i in range(2)]
    u_pairs = [yr1[i] for i in range(2)]
    for a in range(2):
        for direction, chunk, r, keep in ((0, 0, 0, wxlo), (1, CHUNKS - 1, SUB - 1, wxhi)):
            kg = x_ghost(xr1[direction], a, direction, 2)
            ug = x_ghost(xr1[direction], a, direction, 0)
            w = harmonic(perm[a, chunk, r : r + 1, :], kg)
            keep[a : a + 1, :] = w
            dg[a, chunk, r : r + 1, :] += w
            g[a, chunk, r : r + 1, :] += w * ug
        kg = y_ghost(k_high, k_pairs, a, 0)
        ug = y_ghost(u_high, u_pairs, a, 0)
        w = jnp.where(lane128 < 32, harmonic(k_low[a], kg), 0.0)
        wylo[a] = w
        dg[a, :, :, 0:128] += w
        g[a, :, :, 0:128] += w * ug
        kg = y_ghost(k_low, k_pairs, a, 1)
        ug = y_ghost(u_low, u_pairs, a, 1)
        w = jnp.where(lane128 < 32, harmonic(k_high[a], kg), 0.0)
        wyhi[a] = w
        dg[a, :, :, LANES - 128 : LANES] += pltpu.roll(w, 96, 2)
        g[a, :, :, LANES - 128 : LANES] += pltpu.roll(w * ug, 96, 2)

    def first_update(k, _):
        for a in range(2):
            i = OMEGA / dg[a, k]
            inv[a, k] = i
            u1[a, k] = (1.0 - OMEGA) * u0[a, k] + i * g[a, k]
        return 0

    lax.fori_loop(0, CHUNKS, first_update, 0)

    def exchange(number, field, xs, ys, xr, yr):
        fill_x(xs, 0, field)
        faces = y_faces(field)
        for side, minus in enumerate((low_is_minus, high_is_minus)):
            ys[side] = fold(pair_for(faces, minus))
        return send_round(number, xs, ys, xr, yr)

    def correct(field, copies, xr, yr):
        for copy in copies:
            copy.wait_recv()
        low, high = y_faces(field)
        pairs = [unfold(yr[i]) for i in range(2)]
        for a in range(2):
            g[a, 0, 0:1, :] += wxlo[a : a + 1, :] * x_ghost(xr[0], a, 0, 0)
            g[a, CHUNKS - 1, SUB - 1 : SUB, :] += wxhi[a : a + 1, :] * x_ghost(xr[1], a, 1, 0)
            g[a, :, :, 0:128] += wylo[a] * y_ghost(high, pairs, a, 0)
            g[a, :, :, LANES - 128 : LANES] += pltpu.roll(
                wyhi[a] * y_ghost(low, pairs, a, 1), 96, 2
            )

    sent2 = exchange(1, u1, xs2, ys2, xr2, yr2)
    neighbour_sum(u1)
    correct(u1, sent2, xr2, yr2)

    def second_update(k, _):
        for a in range(2):
            u2[a, k] = (1.0 - OMEGA) * u1[a, k] + inv[a, k] * g[a, k]
        return 0

    lax.fori_loop(0, CHUNKS, second_update, 0)
    sent3 = exchange(2, u2, xs3, ys3, xr3, yr3)
    store = pltpu.make_async_copy(u2, out_hbm, out_sem.at[0])
    store.start()
    neighbour_sum(u2)
    correct(u2, sent3, xr3, yr3)

    def residual(k, _):
        for a in range(2):
            at_row = pl.multiple_of(a * 32 + k * SUB, SUB)
            r = g[a, k] - dg[a, k] * u2[a, k]
            for t in range(8):
                res[t, pl.ds(at_row, SUB), :] = r[:, 128 * t : 128 * t + 128]
        return 0

    lax.fori_loop(0, CHUNKS, residual, 0)
    paired = [
        0.125 * (res[t, pl.ds(0, 32, stride=2), :] + res[t, pl.ds(1, 32, stride=2), :])
        for t in range(8)
    ]
    stacked = jnp.concatenate(
        [jnp.concatenate(paired[4 * h : 4 * h + 4], axis=1) for h in range(2)], axis=0
    )
    pooled = jnp.dot(
        stacked, pool[...], preferred_element_type=F32, precision=lax.Precision.HIGHEST
    )
    for a in range(2):
        for t in range(2):
            gathered[my_y, a, :, 128 * t : 128 * t + 128] = pooled[
                32 * t + 16 * a : 32 * t + 16 * a + 16, :
            ]

    spread = [
        remote(
            gathered.at[my_y], gathered.at[my_y], gs_sem.at[o], gr_sem.at[o], device
        )
        for o, device in enumerate(y_peers)
    ]
    for copy in want_copies:
        copy.wait_recv()
    for copy in spread:
        copy.wait_recv()

    shape = (n_y, 2, 16, 256)
    piece_id = (
        (lax.broadcasted_iota(jnp.int32, shape, 0) * 4 + zh * 2 + core) * 2
        + lax.broadcasted_iota(jnp.int32, shape, 1)
    )

    def own(holder, j):
        w = wants[holder, 4 * j : 4 * j + 1, :]
        w = jnp.concatenate([w, w], axis=1).reshape(1, 1, 1, 256)
        return jnp.sum(jnp.where(piece_id == w, gathered[...], 0.0), axis=(0, 1))

    for slot, holder in enumerate((1, 3)):
        for j in range(2):
            sib_out[2 * slot + j] = own(holder, j)
    to_sib = remote(sib_out, sib_in, es_sem.at[0], er_sem.at[0], sib)
    for j in range(2):
        zp_out[j] = own(2, j)
        coarse[j] = own(0, j)
    to_sib.wait_recv()
    for j in range(2):
        zp_out[j] += sib_in[2 + j]
    to_zpar = remote(zp_out, zp_in, es_sem.at[1], er_sem.at[1], zpar)
    for j in range(2):
        coarse[j] += sib_in[j]
    to_zpar.wait_recv()
    for j in range(2):
        coarse[j] += zp_in[j]
    last = pltpu.make_async_copy(coarse, coarse_hbm, out_sem.at[1])
    last.start()
    for copy in sent + want_copies + sent2 + sent3 + spread + [to_sib, to_zpar]:
        copy.wait_send()
    store.wait()
    last.wait()


def body(pressure, source, perm, brinkman, depth_source, sideways, edge_blocks, restrict_take):
    big = (2, CHUNKS, SUB, LANES)
    n_y = lax.axis_size("inslab") // 4
    vm = lambda *shape: pltpu.VMEM(shape, F32)
    dma = lambda n: pltpu.SemaphoreType.DMA((n,))
    anywhere = pl.BlockSpec(memory_space=pltpu.HBM)
    scalars = pl.BlockSpec(memory_space=pltpu.SMEM)
    smoothed, coarse = pl.pallas_call(
        kernel,
        out_shape=(
            jax.ShapeDtypeStruct(big, F32),
            jax.ShapeDtypeStruct((2, 16, 256), F32),
        ),
        in_specs=[anywhere] * 3 + [scalars] * 5,
        out_specs=(anywhere, anywhere),
        scratch_shapes=[vm(*big) for _ in range(14)]
        + [
            vm(2, LANES), vm(2, LANES),
            vm(2, CHUNKS, SUB, 128), vm(2, CHUNKS, SUB, 128),
            vm(8, 64, 128), vm(512, 128),
            vm(2, 4, LANES), vm(2, 2, LANES), vm(2, 2, LANES),
            vm(2, 4, LANES), vm(2, 2, LANES), vm(2, 2, LANES),
            vm(2, 4, SUB, 128), vm(2, 2, SUB, 128), vm(2, 2, SUB, 128),
            vm(2, 4, SUB, 128), vm(2, 2, SUB, 128), vm(2, 2, SUB, 128),
            pltpu.VMEM((4, SUB, 128), jnp.int32),
            vm(n_y, 2, 16, 256),
            vm(4, 16, 256), vm(4, 16, 256), vm(2, 16, 256), vm(2, 16, 256), vm(2, 16, 256),
            dma(3), dma(2), dma(12), dma(12), dma(3), dma(3), dma(n_y - 1), dma(n_y - 1),
            dma(2), dma(2),
        ],
        compiler_params=pltpu.CompilerParams(
            collective_id=0, has_side_effects=True, vmem_limit_bytes=62 * 1024 * 1024
        ),
    )(
        pressure.reshape(big), source.reshape(big), perm.reshape(big), brinkman,
        depth_source, sideways, edge_blocks, restrict_take,
    )
    return smoothed.reshape(pressure.shape), coarse


def solution(mesh):
    group = ("depth", "inslab")
    return jax.shard_map(
        body,
        mesh=mesh,
        in_specs=(
            P(group, None, None),
            P(group, None, None),
            P(group, None, None),
            P(group),
            P(group, None),
            P(group, None),
            P(group, None, None),
            P(group),
        ),
        out_specs=(P(group, None, None), P(group, None, None)),
        check_vma=False,
    )
```

time: 261 us -> 59.3 us (0.23)
  the two profiles are of different devices: /device:TPU:7 before, /device:TPU:1 now
where the time goes in v1:
time: 59.3 us; the launch traced here: 59.1 us
  Pallas kernels  56.2 us (95%)
  local copies, waits for them, and re-layouts  2.3 us (4%)
  between operations  0.65 us (1%)
    pallas_call x1, Pallas kernels, body(): pl.pallas_call(kernel, out_shape=(jax.ShapeDtypeStruct(big, F32), jax.Sha...  56.2 us
    unnamed x4, local copies, waits for them, and re-layouts  2.3 us

profile of v1, /device:TPU:1, one launch (start us, length us, event | category | flops | bytes accessed | tf_op | source)
XLA Modules:
  0.0 59.1 jit_solution(9546453502216105490)
XLA Ops:
  0.6 56.2 %shard_map.95 = (f32[2,4,8,1024]{3,2,1,0:T(8,128)}, f32[2,16,256]{2,1,0:T(8,128)}) custom-call(f32[2,4,8,1024]{3,2,1,0:T(8,128)} %bitcast.4, f32[2,4,8,1024]{3,2,1,0:T(8,128)} %bitcast.5, f32[2,4,8,1024]{3,2,1,0:T(8,128)} %bitcast.6, f32[2]{0:T(128)} %brink.1, s32[2,2]{1,0:T(2,128)} %ds.1, s32[2,4]{1,0:T(2,128)} %snt.1, s32[1,2,2]{2,1,0:T(2,128)} %eb.1, s32[2]{0:T(128)} %take.1), custom_call_target="tpu_custom_call" | custom-call | tf_op jit(solution)/shard_map/pallas_call | solution.py:374
  56.8 0.0 copy-start
  56.8 1.7 %copy.12 = f32[2,32,1024]{2,1,0:T(8,128)} copy(f32[2,32,1024]{2,1,0:T(8,128)} %bitcast.7) | data formatting | bytes 524288
  58.5 0.0 copy-done
  58.5 0.6 %copy.13 = f32[2,16,256]{2,1,0:T(8,128)} copy(f32[2,16,256]{2,1,0:T(8,128)S(1)} %copy-done) | data formatting | bytes 65536
Async XLA Ops:
  56.8 1.7 %copy-start = (f32[2,16,256]{2,1,0:T(8,128)S(1)}, f32[2,16,256]{2,1,0:T(8,128)}, u32[]{:S(2)}) copy-start(f32[2,16,256]{2,1,0:T(8,128)} %get-tuple-element.9) | copy-start | bytes 98308

commit v2 on v1

v2 whole, which is shorter than its diff:
```python
import jax
import jax.numpy as jnp
from jax import lax
from jax.experimental import pallas as pl
from jax.experimental.pallas import tpu as pltpu
from jax.sharding import PartitionSpec as P

OMEGA = 0.8
MESH = pl.DeviceIdType.MESH
F32 = jnp.float32
I32 = jnp.int32
CHUNKS, SUB, LANES = 4, 8, 1024
LAST = LANES - 128


def harmonic(a, b):
    return 2.0 * a * b / (a + b)


def kernel(
    p_hbm, s_hbm, k_hbm, brink_hbm, ds_hbm, snt_hbm, eb_hbm, take_hbm,
    out_hbm, coarse_hbm,
    brink, ds, snt, eb, take,
    u0, src, perm, u1, u2, g, dg, inv, wxm, wxp, wym, wyp, wzm, wzp,
    wxe, wye, res, pool, pool_face,
    xs, xr, ys, yr, edge_out, edge_in,
    tables, face_sum, gathered, x_out, x_in, sib_out, sib_in, zp_out, zp_in, coarse,
    in_sem, out_sem, hs_sem, hr_sem, ts_sem, tr_sem, gs_sem, gr_sem, xs_sem, xr_sem, es_sem, er_sem,
):
    depth = lax.axis_index("depth")
    me = lax.axis_index("inslab")
    n_depth = lax.axis_size("depth")
    n_in = lax.axis_size("inslab")
    n_y = n_in // 4
    my_y = me // 4
    zh = (me // 2) % 2
    core = me % 2

    def at(d, y, z, c):
        return (d, (y * 2 + z) * 2 + c)

    deeper = [lax.rem(depth + n_depth - 1, n_depth), lax.rem(depth + 1, n_depth)]
    beside_me = [lax.rem(me + n_in - 1, n_in), lax.rem(me + 1, n_in)]
    row_peers = [
        at(depth, my_y, zh, 1 - core), at(depth, my_y, 1 - zh, core), at(depth, my_y, 1 - zh, 1 - core)
    ]
    y_peers = [at(depth, lax.rem(my_y + o, n_y), zh, core) for o in range(1, n_y)]
    x_peers = [
        [at(deeper[side], lax.rem(my_y + o, n_y), zh, core) for o in range(n_y)] for side in range(2)
    ]
    i_peers = [(depth, m) for m in beside_me]
    d_peers = [(d, me) for d in deeper]
    corners = [[(d, m) for m in beside_me] for d in deeper]

    has = [depth > 0, depth < n_depth - 1]

    barrier = pltpu.get_barrier_semaphore()

    def greet(partner):
        pl.semaphore_signal(barrier, inc=1, device_id=partner, device_id_type=MESH)

    always = i_peers + row_peers + y_peers
    for partner in always:
        greet(partner)
    for side in range(2):
        pl.when(has[side])(lambda side=side: [greet(p) for p in [d_peers[side]] + corners[side]] and None)
    greeted = len(always) + sum(jnp.where(has[side], 1 + len(corners[side]), 0) for side in range(2))

    small = [(snt_hbm, snt), (ds_hbm, ds), (eb_hbm, eb), (take_hbm, take), (brink_hbm, brink)]
    loads = [
        pltpu.make_async_copy(h, v, in_sem.at[i])
        for i, (h, v) in enumerate([(k_hbm, perm), (p_hbm, u0), (s_hbm, src)] + small)
    ]
    for load in loads:
        load.start()
    for load in loads[3:]:
        load.wait()

    lane3 = lax.broadcasted_iota(I32, (CHUNKS, SUB, 128), 2)
    lane1 = lax.broadcasted_iota(I32, (1, 128), 1)
    row = lax.broadcasted_iota(I32, (SUB, LANES), 0)
    lane = lax.broadcasted_iota(I32, (SUB, LANES), 1)
    zpos = lane % 32
    quarter3 = lane3 // 32
    quarter1 = lane1 // 32

    def remote(a, b, s, r, device):
        copy = pltpu.make_async_remote_copy(
            src_ref=a, dst_ref=b, send_sem=s, recv_sem=r, device_id=device, device_id_type=MESH
        )
        copy.start()
        return copy

    class Link:
        def __init__(self, a, b, s, r, device, side):
            self.args, self.side = (a, b, s, r, device), side
            pl.when(has[side])(lambda: self.make().start())

        def make(self):
            a, b, s, r, device = self.args
            return pltpu.make_async_remote_copy(
                src_ref=a, dst_ref=b, send_sem=s, recv_sem=r, device_id=device, device_id_type=MESH
            )

        def wait_recv(self):
            pl.when(has[1 - self.side])(lambda: self.make().wait_recv())

        def wait_send(self):
            pl.when(has[self.side])(lambda: self.make().wait_send())

    def lies_minus(low):
        found = []
        for a in range(2):
            w = snt[a, 0]
            below = w - 2 < 2 * me
            found.append((w >= 2) & (below if low else jnp.logical_not(below)))
        return found[0] | found[1]

    minus = [lies_minus(True), lies_minus(False)]

    def quarter_of(a, direction):
        w = snt[a, direction]
        column = w & 1
        q = jnp.where(w - 2 < 2 * me, column, 2 + column)
        return jnp.where(w >= 2, q, -1)

    codes = [[quarter_of(a, direction) for direction in range(2)] for a in range(2)]

    trow = lax.broadcasted_iota(I32, (SUB, 128), 0)

    def as_rows(entries):
        tile = jnp.zeros((SUB, 128), I32)
        for i, value in enumerate(entries):
            tile = jnp.where(trow == i, value, tile)
        return tile

    tables[0] = as_rows([take[0], take[1]] + [codes[a][s] for a in range(2) for s in range(2)])
    links = as_rows(
        [ds[a, s] for a in range(2) for s in range(2)]
        + [eb[0, s, c] for s in range(2) for c in range(2)]
    ).astype(F32)

    def y_faces(field):
        low = [field[a, :, :, 0:128] for a in range(2)]
        high = [pltpu.roll(field[a, :, :, LAST:LANES], 32, 2) for a in range(2)]
        return low, high

    def pair_for(faces, is_minus):
        low, high = faces
        cols = []
        for c in range(2):
            from_low = jnp.where(eb[0, 0, c] == 1, low[1], low[0])
            from_high = jnp.where(eb[0, 1, c] == 1, high[1], high[0])
            cols.append(jnp.where(is_minus, from_low, from_high))
        return jnp.where(lane3 < 32, cols[0], pltpu.roll(cols[1], 32, 2))

    def x_face(field, side, a):
        if side == 0:
            return field[a, 0, 0:1, :]
        return field[a, CHUNKS - 1, SUB - 1 : SUB, :]

    def fill(first, second, block):
        for side in range(2):
            for a in range(2):
                n = 4 * block + a
                xs[side, n : n + 1, :] = x_face(first, side, a)
                xs[side, n + 2 : n + 3, :] = x_face(second, side, a)
        one, two = y_faces(first), y_faces(second)
        for peer in range(2):
            ys[peer, CHUNKS * block : CHUNKS * block + CHUNKS] = jnp.where(
                lane3 < 64, pair_for(one, minus[peer]), pltpu.roll(pair_for(two, minus[peer]), 64, 2)
            )

    loads[0].wait()
    loads[1].wait()
    fill(u0, perm, 0)
    for peer in range(2):
        ys[peer, 2 * CHUNKS] = links
    for side in range(2):
        for f, field in enumerate((u0, perm)):
            lines = []
            for a in range(2):
                face = x_face(field, side, a)
                lines.append([face[:, 0:128], pltpu.roll(face[:, LAST:LANES], 32, 1)])
            by_column = [
                jnp.where(eb[0, s, c] == 1, lines[1][s], lines[0][s]) for s in range(2) for c in range(2)
            ]
            by_slot = [lines[a][s] for a in range(2) for s in range(2)]
            for n, listed in enumerate((by_column, by_slot)):
                packed = listed[0]
                for q in range(1, 4):
                    packed = jnp.where(quarter1 == q, pltpu.roll(listed[q], 32 * q, 1), packed)
                edge_out[side, 2 * n + f : 2 * n + f + 1, :] = packed
    def zslot(a, direction):
        return jnp.maximum(snt[a, 2 + direction], 0)

    def beside(field, a, k):
        u = field[a, k]
        before = field[a, jnp.maximum(k - 1, 0), SUB - 1 : SUB, :]
        after = field[a, jnp.minimum(k + 1, CHUNKS - 1), 0:1, :]
        um = jnp.where(row == 0, before, pltpu.roll(u, 1, 0))
        up = jnp.where(row == SUB - 1, after, pltpu.roll(u, SUB - 1, 0))
        ym = pltpu.roll(u, 32, 1)
        yp = pltpu.roll(u, LANES - 32, 1)
        nm = field[zslot(a, 0), k]
        np_ = field[zslot(a, 1), k]
        zm = jnp.where(zpos == 0, pltpu.roll(nm, LANES - 31, 1), pltpu.roll(u, 1, 1))
        zp = jnp.where(zpos == 31, pltpu.roll(np_, 31, 1), pltpu.roll(u, LANES - 1, 1))
        return u, (um, up, ym, yp, zm, zp)

    def weights(k, _):
        for a in range(2):
            kk, nbs = beside(perm, a, k)
            has_zm = snt[a, 2] >= 0
            has_zp = snt[a, 3] >= 0
            keep = (
                jnp.logical_not((row == 0) & (k == 0)),
                jnp.logical_not((row == SUB - 1) & (k == CHUNKS - 1)),
                lane >= 32,
                lane < LANES - 32,
                jnp.logical_or(zpos != 0, has_zm),
                jnp.logical_or(zpos != 31, has_zp),
            )
            total = jnp.full((SUB, LANES), brink[a], F32)
            for store, nb, mask in zip((wxm, wxp, wym, wyp, wzm, wzp), nbs, keep):
                w = jnp.where(mask, harmonic(kk, nb), 0.0)
                store[a, k] = w
                total = total + w
            dg[a, k] = total
        return 0

    lax.fori_loop(0, CHUNKS, weights, 0)
    loads[2].wait()

    def neighbour_sum(field):
        def step(k, _):
            for a in range(2):
                _, nbs = beside(field, a, k)
                total = src[a, k]
                for store, nb in zip((wxm, wxp, wym, wyp, wzm, wzp), nbs):
                    total = total + store[a, k] * nb
                g[a, k] = total
            return 0

        lax.fori_loop(0, CHUNKS, step, 0)

    neighbour_sum(u0)
    fill(g, dg, 1)

    pl.semaphore_wait(barrier, greeted)
    sent = []
    for peer in range(2):
        sent.append(remote(ys.at[peer], yr.at[1 - peer], hs_sem.at[peer], hr_sem.at[peer], i_peers[peer]))
    for side in range(2):
        for peer in range(2):
            n = 4 + 2 * side + peer
            sent.append(
                Link(
                    edge_out.at[side], edge_in.at[1 - side, 1 - peer],
                    hs_sem.at[n], hr_sem.at[n], corners[side][peer], side,
                )
            )
    for side in range(2):
        n = 2 + side
        sent.append(
            Link(xs.at[side], xr.at[1 - side], hs_sem.at[n], hr_sem.at[n], d_peers[side], side)
        )
        sent.append(
            Link(
                tables.at[0], tables.at[2 - side], ts_sem.at[side], tr_sem.at[side], d_peers[side], side
            )
        )
    wants = [
        remote(tables.at[0], tables.at[3 + j], ts_sem.at[2 + j], tr_sem.at[2 + j], device)
        for j, device in enumerate(row_peers)
    ]

    prow = lax.broadcasted_iota(I32, (512, 128), 0)
    pcol = lax.broadcasted_iota(I32, (512, 128), 1)
    pool[...] = 0.125 * ((prow // 64) * 16 + (prow % 32) // 2 == pcol).astype(F32)
    frow = lax.broadcasted_iota(I32, (256, 128), 0)
    fcol = lax.broadcasted_iota(I32, (256, 128), 1)
    spot = (frow % 128) // 32 * 32 + (1 - frow // 128) * 16 + (frow % 32) // 2
    pool_face[...] = 0.125 * (spot == fcol).astype(F32)

    def pick(choice, options):
        found = jnp.zeros_like(options[0])
        for i, option in enumerate(options):
            found = jnp.where(choice == i, option, found)
        return found

    for side in range(2):

        @pl.when(jnp.logical_not(has[side]))
        def _():
            xr[side] = jnp.ones((8, LANES), F32)
            x_in[side] = jnp.zeros((n_y, 2, 2, 128), F32)
            tables[1 + side] = jnp.full((SUB, 128), -1, I32)
            for peer in range(2):
                edge_in[side, peer] = jnp.zeros((4, 128), F32)

    for copy in sent:
        copy.wait_recv()

    px, kx, gx, dx = (
        [[xr[s, n + j : n + j + 1, :] for j in range(2)] for s in range(2)] for n in (0, 2, 4, 6)
    )

    def both(block):
        low, high = [yr[peer, CHUNKS * block : CHUNKS * block + CHUNKS] for peer in range(2)]
        return (
            jnp.where(lane3 < 64, low, pltpu.roll(high, 64, 2)),
            jnp.where(lane3 < 64, pltpu.roll(low, 64, 2), high),
        )

    py, ky = both(0)
    gy, dy = both(1)

    def rotated(quarters):
        return [quarters] + [pltpu.roll(quarters, 128 - 32 * q, 2) for q in range(1, 4)]

    def own_faces(field):
        low, high = y_faces(field)
        return [[low[a], high[a]] for a in range(2)]

    def into_quarters(faces, keys):
        total = jnp.zeros((CHUNKS, SUB, 128), F32)
        for a in range(2):
            for direction in range(2):
                face = jnp.where(lane3 < 32, faces[a][direction], 0.0)
                face = face + pltpu.roll(face, 32, 2)
                face = face + pltpu.roll(face, 64, 2)
                total = total + jnp.where(quarter3 == keys[a][direction], face, 0.0)
        return total

    k_faces, u_faces = own_faces(perm), own_faces(u0)
    k_turned, u_turned = rotated(ky), rotated(py)

    def add_y(ref, a, direction, value):
        if direction == 0:
            ref[a, :, :, 0:128] += value
        else:
            ref[a, :, :, LAST:LANES] += pltpu.roll(value, 96, 2)

    def add_x(ref, a, side, value):
        if side == 0:
            ref[a, 0, 0:1, :] += value
        else:
            ref[a, CHUNKS - 1, SUB - 1 : SUB, :] += value

    for a in range(2):
        for side in range(2):
            w = harmonic(x_face(perm, side, a), pick(ds[a, side], kx[side]))
            wxe[side, a : a + 1, :] = w
            add_x(dg, a, side, w)
            add_x(g, a, side, w * pick(ds[a, side], px[side]))
        for direction in range(2):
            kg = pick(codes[a][direction], k_turned)
            w = jnp.where(lane3 < 32, harmonic(k_faces[a][direction], kg), 0.0)
            wye[a, direction] = w
            add_y(dg, a, direction, w)
            add_y(g, a, direction, w * pick(codes[a][direction], u_turned))

    def line(packed, start, target):
        return pltpu.roll(packed, (target - start) % 4 * 32, 1) if start != target else packed

    px1 = []
    for side in range(2):
        found = []
        for j in range(2):
            gsum, dsum = gx[side][j], dx[side][j]
            mine_p = jnp.zeros((1, LANES), F32)
            mine_k = jnp.zeros((1, LANES), F32)
            for a in range(2):
                linked = ds[a, side] == j
                mine_p = jnp.where(linked, x_face(u0, side, a), mine_p)
                mine_k = jnp.where(linked, x_face(perm, side, a), mine_k)
            w = harmonic(kx[side][j], mine_k)
            gsum = gsum + w * mine_p
            dsum = dsum + w
            ends = []
            for direction in range(2):
                code = tables[1 + side, 2 + 2 * j + direction : 3 + 2 * j + direction, :]
                start = 2 if direction == 0 else 0
                target = 0 if direction == 0 else 3
                values = []
                for f in range(2):
                    options = [
                        line(edge_in[side, peer, f : f + 1, :], start + c, target)
                        for peer in range(2)
                        for c in range(2)
                    ]
                    values.append(pick(code, options))
                kk = kx[side][j][:, 0:128] if direction == 0 else kx[side][j][:, LAST:LANES]
                w = jnp.where(quarter1 == target, harmonic(kk, values[1]), 0.0)
                ends.append((w, w * values[0]))
            gap = jnp.zeros((1, LANES - 256), F32)
            dsum = dsum + jnp.concatenate([ends[0][0], gap, ends[1][0]], axis=1)
            gsum = gsum + jnp.concatenate([ends[0][1], gap, ends[1][1]], axis=1)
            found.append((1.0 - OMEGA) * px[side][j] + OMEGA * gsum / dsum)
        px1.append(found)

    mine_k = into_quarters(k_faces, codes)
    w = harmonic(ky, mine_k)
    gy = gy + w * into_quarters(u_faces, codes)
    dy = dy + w
    slots = []
    for peer in range(2):
        held = yr[peer, 2 * CHUNKS]
        for c in range(2):
            slots.append(jnp.where(minus[peer], held[6 + c : 7 + c, :], held[4 + c : 5 + c, :]))
    rows3 = lax.broadcasted_iota(I32, (CHUNKS, SUB, 128), 0) * SUB + lax.broadcasted_iota(
        I32, (CHUNKS, SUB, 128), 1
    )
    for side in range(2):
        values = []
        for f in range(2):
            total = jnp.zeros((1, 128), F32)
            for q in range(4):
                peer = q // 2
                held = yr[peer, 2 * CHUNKS]
                link = jnp.where(
                    slots[q] == 1, held[2 + side : 3 + side, :], held[side : side + 1, :]
                )
                edge = edge_in[side, peer, 2 + f : 3 + f, :]
                options = [
                    jnp.where(minus[peer], line(edge, 2 * s + 1, q), line(edge, 2 * s, q))
                    for s in range(2)
                ]
                total = jnp.where(quarter1 == q, pick(link, options), total)
            values.append(total)
        r = 0 if side == 0 else CHUNKS * SUB - 1
        here = ky[0, 0:1, :] if side == 0 else ky[CHUNKS - 1, SUB - 1 : SUB, :]
        w = harmonic(here, values[1])
        dy = dy + jnp.where(rows3 == r, w.reshape(1, 1, 128), 0.0)
        gy = gy + jnp.where(rows3 == r, (w * values[0]).reshape(1, 1, 128), 0.0)
    py1 = (1.0 - OMEGA) * py + OMEGA * gy / dy

    def first_update(k, _):
        for a in range(2):
            i = OMEGA / dg[a, k]
            inv[a, k] = i
            u1[a, k] = (1.0 - OMEGA) * u0[a, k] + i * g[a, k]
        return 0

    lax.fori_loop(0, CHUNKS, first_update, 0)
    neighbour_sum(u1)
    u_turned = rotated(py1)
    for a in range(2):
        for side in range(2):
            add_x(g, a, side, wxe[side, a : a + 1, :] * pick(ds[a, side], px1[side]))
        for direction in range(2):
            add_y(g, a, direction, wye[a, direction] * pick(codes[a][direction], u_turned))

    def second_update(k, _):
        for a in range(2):
            u2[a, k] = (1.0 - OMEGA) * u1[a, k] + inv[a, k] * g[a, k]
        return 0

    lax.fori_loop(0, CHUNKS, second_update, 0)
    store = pltpu.make_async_copy(u2, out_hbm, out_sem.at[0])
    store.start()
    neighbour_sum(u2)

    def residual(k, _):
        for a in range(2):
            at_row = pl.multiple_of(a * 32 + k * SUB, SUB)
            r = g[a, k] - dg[a, k] * u2[a, k]
            for t in range(8):
                res[t, pl.ds(at_row, SUB), :] = r[:, 128 * t : 128 * t + 128]
        return 0

    lax.fori_loop(0, CHUNKS, residual, 0)
    paired = [
        res[t, pl.ds(0, 32, stride=2), :] + res[t, pl.ds(1, 32, stride=2), :] for t in range(8)
    ]
    stacked = [jnp.concatenate(paired[4 * h : 4 * h + 4], axis=1) for h in range(2)]

    across = []
    for side in range(2):
        flows = [wxe[side, a : a + 1, :] * x_face(u2, side, a) for a in range(2)]
        for s in range(2):
            total = jnp.zeros((1, LANES), F32)
            for a in range(2):
                total = total + jnp.where(ds[a, side] == s, flows[a], 0.0)
            across.append(total)
    across = jnp.concatenate(across, axis=0)
    stacked += [across[:, 0:512], across[:, 512:1024]]
    pooled = jnp.dot(
        jnp.concatenate(stacked, axis=0), pool[...],
        preferred_element_type=F32, precision=lax.Precision.HIGHEST,
    )
    for a in range(2):
        for t in range(2):
            gathered[my_y, 2 * a + t] = pooled[32 * t + 16 * a : 32 * t + 16 * a + 16, :]
    for side in range(2):
        for t in range(2):
            x_out[side, t] = pooled[64 + 4 * t + 2 * side : 66 + 4 * t + 2 * side, :]

    u_faces = own_faces(u2)
    for direction in range(2):
        total = jnp.zeros((CHUNKS, SUB, 128), F32)
        for a in range(2):
            face = wye[a, direction] * u_faces[a][direction]
            face = face + pltpu.roll(face, 32, 2)
            face = face + pltpu.roll(face, 64, 2)
            code = codes[a][direction]
            slot = pick(code, slots)
            key = jnp.where(code >= 2, 2.0, 0.0) + slot
            hit = (quarter1.astype(F32) == key) & (code >= 0)
            total = total + jnp.where(hit.reshape(1, 1, 128), face, 0.0)
        face_sum[direction] = total.reshape(CHUNKS * SUB, 128)
    halves = []
    for direction in range(2):
        even = face_sum[direction, pl.ds(0, 16, stride=2), :]
        halves.append(even + face_sum[direction, pl.ds(1, 16, stride=2), :])
    gathered[my_y, 4] = jnp.dot(
        jnp.concatenate(halves, axis=1), pool_face[...],
        preferred_element_type=F32, precision=lax.Precision.HIGHEST,
    )

    spread = [
        remote(gathered.at[my_y], gathered.at[my_y], gs_sem.at[o], gr_sem.at[o], device)
        for o, device in enumerate(y_peers)
    ]
    for side in range(2):
        for o, device in enumerate(x_peers[side]):
            n = side * n_y + o
            spread.append(
                Link(x_out.at[side], x_in.at[1 - side, my_y], xs_sem.at[n], xr_sem.at[n], device, side)
            )
    for copy in wants:
        copy.wait_recv()
    for copy in spread:
        copy.wait_recv()

    def device_at(y):
        return (y * 2 + zh) * 2 + core

    piece = (n_y, 2, 16, 128)
    piece_id = device_at(lax.broadcasted_iota(I32, piece, 0)) * 2 + lax.broadcasted_iota(I32, piece, 1)
    x_shape = (n_y, 2, 128)
    x_id = device_at(lax.broadcasted_iota(I32, x_shape, 0)) * 2 + lax.broadcasted_iota(I32, x_shape, 1)
    y_shape = (n_y, 16, 128)
    y_lane = lax.broadcasted_iota(I32, y_shape, 2)
    y_id = (device_at(lax.broadcasted_iota(I32, y_shape, 0)) + 2 * (y_lane // 64) - 1) * 2 + (
        y_lane % 64
    ) // 32
    lane2 = lax.broadcasted_iota(I32, (16, 128), 1)
    row2 = lax.broadcasted_iota(I32, (16, 128), 0)

    def own(holder, j, out, at_slot):
        w = tables[holder, j : j + 1, :]
        w3, w4 = w.reshape(1, 1, 128), w.reshape(1, 1, 1, 128)
        y_part = jnp.sum(jnp.where(y_id == w3, gathered[:, 4], 0.0), axis=0)
        y_part = y_part + pltpu.roll(y_part, 64, 1)
        y_part = y_part + pltpu.roll(y_part, 32, 1)
        for t in range(2):
            held = jnp.stack([gathered[:, t], gathered[:, 2 + t]], axis=1)
            found = jnp.sum(jnp.where(piece_id == w4, held, 0.0), axis=(0, 1))
            found = found + jnp.where(lane2 < 16 if t == 0 else lane2 >= 112, y_part, 0.0)
            for side in range(2):
                x_part = jnp.sum(
                    jnp.where(x_id == w3, x_in[side, :, t], 0.0), axis=(0, 1)
                ).reshape(1, 128)
                found = found + jnp.where(row2 == (0 if side == 0 else 15), x_part, 0.0)
            out[at_slot, :, 128 * t : 128 * t + 128] = found

    for slot, holder in enumerate((3, 5)):
        for j in range(2):
            own(holder, j, sib_out, 2 * slot + j)
    to_sib = remote(sib_out, sib_in, es_sem.at[0], er_sem.at[0], row_peers[0])
    for j in range(2):
        own(4, j, zp_out, j)
        own(0, j, coarse, j)
    to_sib.wait_recv()
    for j in range(2):
        zp_out[j] += sib_in[2 + j]
    to_zpar = remote(zp_out, zp_in, es_sem.at[1], er_sem.at[1], row_peers[1])
    for j in range(2):
        coarse[j] += sib_in[j]
    to_zpar.wait_recv()
    for j in range(2):
        coarse[j] += zp_in[j]
    last = pltpu.make_async_copy(coarse, coarse_hbm, out_sem.at[1])
    last.start()
    for copy in sent + wants + spread + [to_sib, to_zpar]:
        copy.wait_send()
    store.wait()
    last.wait()


def body(pressure, source, perm, brinkman, depth_source, sideways, edge_blocks, restrict_take):
    big = (2, CHUNKS, SUB, LANES)
    n_y = lax.axis_size("inslab") // 4
    vm = lambda *shape: pltpu.VMEM(shape, F32)
    dma = lambda n: pltpu.SemaphoreType.DMA((n,))
    anywhere = pl.BlockSpec(memory_space=pltpu.HBM)
    arrays = [x.reshape(big) for x in (pressure, source, perm)]
    arrays += [brinkman, depth_source, sideways, edge_blocks, restrict_take]
    smoothed, coarse = pl.pallas_call(
        kernel,
        out_shape=(
            jax.ShapeDtypeStruct(big, F32),
            jax.ShapeDtypeStruct((2, 16, 256), F32),
        ),
        in_specs=[anywhere] * 8,
        out_specs=(anywhere, anywhere),
        scratch_shapes=[
            pltpu.SMEM((2,), F32), pltpu.SMEM((2, 2), I32), pltpu.SMEM((2, 4), I32),
            pltpu.SMEM((1, 2, 2), I32), pltpu.SMEM((2,), I32),
        ]
        + [vm(*big) for _ in range(14)]
        + [
            vm(2, 2, LANES), vm(2, 2, CHUNKS, SUB, 128), vm(8, 64, 128), vm(512, 128), vm(256, 128),
            vm(2, 8, LANES), vm(2, 8, LANES),
            vm(2, 2 * CHUNKS + 1, SUB, 128), vm(2, 2 * CHUNKS + 1, SUB, 128),
            vm(2, 4, 128), vm(2, 2, 4, 128),
            pltpu.VMEM((6, SUB, 128), I32),
            vm(2, CHUNKS * SUB, 128),
            vm(n_y, 5, 16, 128), vm(2, 2, 2, 128), vm(2, n_y, 2, 2, 128),
            vm(4, 16, 256), vm(4, 16, 256), vm(2, 16, 256), vm(2, 16, 256), vm(2, 16, 256),
            dma(8), dma(2), dma(8), dma(8), dma(5), dma(5), dma(n_y - 1), dma(n_y - 1),
            dma(2 * n_y), dma(2 * n_y), dma(2), dma(2),
        ],
        compiler_params=pltpu.CompilerParams(
            collective_id=0, has_side_effects=True, vmem_limit_bytes=32 * 1024 * 1024
        ),
    )(*[pltpu.with_memory_space_constraint(x, pltpu.HBM) for x in arrays])
    return smoothed.reshape(pressure.shape), coarse


def solution(mesh):
    group = ("depth", "inslab")
    return jax.shard_map(
        body,
        mesh=mesh,
        in_specs=(
            P(group, None, None),
            P(group, None, None),
            P(group, None, None),
            P(group),
            P(group, None),
            P(group, None),
            P(group, None, None),
            P(group),
        ),
        out_specs=(P(group, None, None), P(group, None, None)),
        check_vma=False,
    )
```

time: 59.3 us -> 51.4 us (0.87)
  the two profiles are of different devices: /device:TPU:1 before, /device:TPU:7 now
where the time goes in v2:
time: 51.4 us; the launch traced here: 51.3 us
  Pallas kernels  49.3 us (96%)
  local copies, waits for them, and re-layouts  1.32 us (3%)
  between operations  0.64 us (1%)
    pallas_call x1, Pallas kernels, body(): pl.pallas_call(kernel, out_shape=(jax.ShapeDtypeStruct(big, F32), jax.Sha...  49.3 us
    unnamed x2, local copies, waits for them, and re-layouts  1.32 us

profile of v2, /device:TPU:7, one launch (start us, length us, event | category | flops | bytes accessed | tf_op | source)
XLA Modules:
  0.0 51.3 jit_solution(14328525909839879910)
XLA Ops:
  0.6 49.3 %shard_map.95 = (f32[2,4,8,1024]{3,2,1,0:T(8,128)S(1)}, f32[2,16,256]{2,1,0:T(8,128)S(1)}) custom-call(f32[2,4,8,1024]{3,2,1,0:T(8,128)} %bitcast.5, f32[2,4,8,1024]{3,2,1,0:T(8,128)} %bitcast.6, f32[2,4,8,1024]{3,2,1,0:T(8,128)} %bitcast.7, f32[2]{0:T(128)} %brink_hbm.1, s32[2,2]{1,0:T(2,128)} %ds_hbm.1, s32[2,4]{1,0:T(2,128)} %snt_hbm.1, ...), custom_call_target="tpu_custom_call" | custom-call | tf_op jit(solution)/shard_map/pallas_call | solution.py:601
  50.0 0.7 %copy.12 = f32[2,32,1024]{2,1,0:T(8,128)} copy(f32[2,32,1024]{2,1,0:T(8,128)S(1)} %bitcast.4) | data formatting | bytes 524288
  50.7 0.6 %copy.13 = f32[2,16,256]{2,1,0:T(8,128)} copy(f32[2,16,256]{2,1,0:T(8,128)S(1)} %get-tuple-element.9) | data formatting | bytes 65536

commit v3 on v2

--- a/solution.py
+++ b/solution.py
@@ -21,11 +21,11 @@
     p_hbm, s_hbm, k_hbm, brink_hbm, ds_hbm, snt_hbm, eb_hbm, take_hbm,
     out_hbm, coarse_hbm,
     brink, ds, snt, eb, take,
-    u0, src, perm, u1, u2, g, dg, inv, wxm, wxp, wym, wyp, wzm, wzp,
+    u0, src, perm, u1, u2, g, ga, dg, inv, wxm, wxp, wym, wyp, wzm, wzp,
     wxe, wye, res, pool, pool_face,
     xs, xr, ys, yr, edge_out, edge_in,
-    tables, face_sum, gathered, x_out, x_in, sib_out, sib_in, zp_out, zp_in, coarse,
-    in_sem, out_sem, hs_sem, hr_sem, ts_sem, tr_sem, gs_sem, gr_sem, xs_sem, xr_sem, es_sem, er_sem,
+    tables, face_sum, bulk, late, x_out, x_in, bulk_out, bulk_in, shell_out, shell_in, coarse,
+    in_sem, out_sem, hs_sem, hr_sem, ts_sem, tr_sem, bs_sem, br_sem, gs_sem, gr_sem, xs_sem, xr_sem, es_sem, er_sem,
 ):
     depth = lax.axis_index("depth")
     me = lax.axis_index("inslab")
@@ -232,21 +232,76 @@
     lax.fori_loop(0, CHUNKS, weights, 0)
     loads[2].wait()
 
-    def neighbour_sum(field):
+    def neighbour_sum(field, into):
         def step(k, _):
             for a in range(2):
                 _, nbs = beside(field, a, k)
                 total = src[a, k]
                 for store, nb in zip((wxm, wxp, wym, wyp, wzm, wzp), nbs):
                     total = total + store[a, k] * nb
-                g[a, k] = total
+                into[a, k] = total
             return 0
 
         lax.fori_loop(0, CHUNKS, step, 0)
 
-    neighbour_sum(u0)
+    neighbour_sum(u0, g)
     fill(g, dg, 1)
 
+    prow = lax.broadcasted_iota(I32, (512, 128), 0)
+    pcol = lax.broadcasted_iota(I32, (512, 128), 1)
+    pool[...] = 0.125 * ((prow // 64) * 16 + (prow % 32) // 2 == pcol).astype(F32)
+    frow = lax.broadcasted_iota(I32, (128, 128), 0)
+    fcol = lax.broadcasted_iota(I32, (128, 128), 1)
+    pool_face[...] = 0.125 * (frow // 32 * 16 + (frow % 32) // 2 == fcol).astype(F32)
+
+    def pooled_residual(field, sums, more):
+        def step(k, _):
+            for a in range(2):
+                at_row = pl.multiple_of(a * 32 + k * SUB, SUB)
+                r = sums[a, k] - dg[a, k] * field[a, k]
+                for t in range(8):
+                    res[t, pl.ds(at_row, SUB), :] = r[:, 128 * t : 128 * t + 128]
+            return 0
+
+        lax.fori_loop(0, CHUNKS, step, 0)
+        paired = [
+            res[t, pl.ds(0, 32, stride=2), :] + res[t, pl.ds(1, 32, stride=2), :] for t in range(8)
+        ]
+        stacked = [jnp.concatenate(paired[4 * h : 4 * h + 4], axis=1) for h in range(2)]
+        return jnp.dot(
+            jnp.concatenate(stacked + more, axis=0), pool[...],
+            preferred_element_type=F32, precision=lax.Precision.HIGHEST,
+        )
+
+    def piece_of(pooled, a, t):
+        return pooled[32 * t + 16 * a : 32 * t + 16 * a + 16, :]
+
+    def inner_first(k, _):
+        for a in range(2):
+            i = OMEGA / dg[a, k]
+            inv[a, k] = i
+            u1[a, k] = (1.0 - OMEGA) * u0[a, k] + i * g[a, k]
+        return 0
+
+    def inner_second(k, _):
+        for a in range(2):
+            u2[a, k] = (1.0 - OMEGA) * u1[a, k] + inv[a, k] * ga[a, k]
+        return 0
+
+    def inner_pieces():
+        lax.fori_loop(0, CHUNKS, inner_first, 0)
+        neighbour_sum(u1, ga)
+        lax.fori_loop(0, CHUNKS, inner_second, 0)
+        neighbour_sum(u2, ga)
+        pooled = pooled_residual(u2, ga, [])
+        for a in range(2):
+            for t in range(2):
+                n = 4 * a + 2 * t
+                bulk[my_y, n : n + 2] = piece_of(pooled, a, t).reshape(2, SUB, 128)
+        sides = jnp.where(quarter1 % 2 == 0, minus[0].astype(F32), minus[1].astype(F32))
+        bulk[my_y, 8] = jnp.broadcast_to(sides, (SUB, 128))
+
+    inner_pieces()
     pl.semaphore_wait(barrier, greeted)
     sent = []
     for peer in range(2):
@@ -274,14 +329,10 @@
         remote(tables.at[0], tables.at[3 + j], ts_sem.at[2 + j], tr_sem.at[2 + j], device)
         for j, device in enumerate(row_peers)
     ]
-
-    prow = lax.broadcasted_iota(I32, (512, 128), 0)
-    pcol = lax.broadcasted_iota(I32, (512, 128), 1)
-    pool[...] = 0.125 * ((prow // 64) * 16 + (prow % 32) // 2 == pcol).astype(F32)
-    frow = lax.broadcasted_iota(I32, (256, 128), 0)
-    fcol = lax.broadcasted_iota(I32, (256, 128), 1)
-    spot = (frow % 128) // 32 * 32 + (1 - frow // 128) * 16 + (frow % 32) // 2
-    pool_face[...] = 0.125 * (spot == fcol).astype(F32)
+    early = [
+        remote(bulk.at[my_y], bulk.at[my_y], bs_sem.at[o], br_sem.at[o], device)
+        for o, device in enumerate(y_peers)
+    ]
 
     def pick(choice, options):
         found = jnp.zeros_like(options[0])
@@ -444,7 +495,7 @@
         return 0
 
     lax.fori_loop(0, CHUNKS, first_update, 0)
-    neighbour_sum(u1)
+    neighbour_sum(u1, g)
     u_turned = rotated(py1)
     for a in range(2):
         for side in range(2):
@@ -460,21 +511,7 @@
     lax.fori_loop(0, CHUNKS, second_update, 0)
     store = pltpu.make_async_copy(u2, out_hbm, out_sem.at[0])
     store.start()
-    neighbour_sum(u2)
-
-    def residual(k, _):
-        for a in range(2):
-            at_row = pl.multiple_of(a * 32 + k * SUB, SUB)
-            r = g[a, k] - dg[a, k] * u2[a, k]
-            for t in range(8):
-                res[t, pl.ds(at_row, SUB), :] = r[:, 128 * t : 128 * t + 128]
-        return 0
-
-    lax.fori_loop(0, CHUNKS, residual, 0)
-    paired = [
-        res[t, pl.ds(0, 32, stride=2), :] + res[t, pl.ds(1, 32, stride=2), :] for t in range(8)
-    ]
-    stacked = [jnp.concatenate(paired[4 * h : 4 * h + 4], axis=1) for h in range(2)]
+    neighbour_sum(u2, g)
 
     across = []
     for side in range(2):
@@ -485,14 +522,17 @@
                 total = total + jnp.where(ds[a, side] == s, flows[a], 0.0)
             across.append(total)
     across = jnp.concatenate(across, axis=0)
-    stacked += [across[:, 0:512], across[:, 512:1024]]
-    pooled = jnp.dot(
-        jnp.concatenate(stacked, axis=0), pool[...],
-        preferred_element_type=F32, precision=lax.Precision.HIGHEST,
-    )
+    pooled = pooled_residual(u2, g, [across[:, 0:512], across[:, 512:1024]])
+    lane2 = lax.broadcasted_iota(I32, (16, 128), 1)
+    edges = jnp.zeros((16, 128), F32)
     for a in range(2):
         for t in range(2):
-            gathered[my_y, 2 * a + t] = pooled[32 * t + 16 * a : 32 * t + 16 * a + 16, :]
+            part = piece_of(pooled, a, t)
+            late[my_y, a, 4 * t : 4 * t + 2, :] = part[0:2, :]
+            late[my_y, a, 4 * t + 2 : 4 * t + 4, :] = part[14:16, :]
+            part = part if a == t else pltpu.roll(part, 64, 1)
+            edges = jnp.where(lane2 // 32 == 2 * a + t, part, edges)
+    late[my_y, 2:4] = edges.reshape(2, SUB, 128)
     for side in range(2):
         for t in range(2):
             x_out[side, t] = pooled[64 + 4 * t + 2 * side : 66 + 4 * t + 2 * side, :]
@@ -510,17 +550,17 @@
             hit = (quarter1.astype(F32) == key) & (code >= 0)
             total = total + jnp.where(hit.reshape(1, 1, 128), face, 0.0)
         face_sum[direction] = total.reshape(CHUNKS * SUB, 128)
-    halves = []
-    for direction in range(2):
-        even = face_sum[direction, pl.ds(0, 16, stride=2), :]
-        halves.append(even + face_sum[direction, pl.ds(1, 16, stride=2), :])
-    gathered[my_y, 4] = jnp.dot(
-        jnp.concatenate(halves, axis=1), pool_face[...],
+    halves = [
+        face_sum[direction, pl.ds(first, 16, stride=2), :] for direction in range(2) for first in range(2)
+    ]
+    faces = jnp.dot(
+        halves[0] + halves[1] + halves[2] + halves[3], pool_face[...],
         preferred_element_type=F32, precision=lax.Precision.HIGHEST,
     )
+    late[my_y, 4] = jnp.where(lane2[0:8] < 64, faces[0:8], pltpu.roll(faces[8:16], 64, 1))
 
     spread = [
-        remote(gathered.at[my_y], gathered.at[my_y], gs_sem.at[o], gr_sem.at[o], device)
+        remote(late.at[my_y], late.at[my_y], gs_sem.at[o], gr_sem.at[o], device)
         for o, device in enumerate(y_peers)
     ]
     for side in range(2):
@@ -529,62 +569,109 @@
             spread.append(
                 Link(x_out.at[side], x_in.at[1 - side, my_y], xs_sem.at[n], xr_sem.at[n], device, side)
             )
-    for copy in wants:
+    for copy in wants + early:
         copy.wait_recv()
+
+    def device_at(y):
+        return (y * 2 + zh) * 2 + core
+
+    def iota(shape, dim):
+        return lax.broadcasted_iota(I32, shape, dim)
+
+    bulk_shape = (n_y, 2, 4, SUB, 128)
+    bulk_id = device_at(iota(bulk_shape, 0)) * 2 + iota(bulk_shape, 1)
+
+    def want(holder, j):
+        return tables[holder, j : j + 1, :]
+
+    holders = (0, 3, 4, 5)
+    for h in (2, 3, 1, 0):
+        held = bulk[:, 0:8].reshape(bulk_shape)
+        for j in range(2):
+            w = want(holders[h], j).reshape(1, 1, 1, 1, 128)
+            bulk_out[h, 4 * j : 4 * j + 4] = jnp.sum(jnp.where(bulk_id == w, held, 0.0), axis=(0, 1))
+    rows_of_bulk = [
+        remote(bulk_out.at[1 + j], bulk_in.at[j], es_sem.at[j], er_sem.at[j], row_peers[j])
+        for j in (1, 2, 0)
+    ]
+
     for copy in spread:
         copy.wait_recv()
 
-    def device_at(y):
-        return (y * 2 + zh) * 2 + core
-
-    piece = (n_y, 2, 16, 128)
-    piece_id = device_at(lax.broadcasted_iota(I32, piece, 0)) * 2 + lax.broadcasted_iota(I32, piece, 1)
+    a_shape = (n_y, 2, SUB, 128)
+    a_id = device_at(iota(a_shape, 0)) * 2 + iota(a_shape, 1)
+    b_id = device_at(iota(a_shape, 0)) * 2 + iota(a_shape, 3) // 64
     x_shape = (n_y, 2, 128)
-    x_id = device_at(lax.broadcasted_iota(I32, x_shape, 0)) * 2 + lax.broadcasted_iota(I32, x_shape, 1)
-    y_shape = (n_y, 16, 128)
-    y_lane = lax.broadcasted_iota(I32, y_shape, 2)
-    y_id = (device_at(lax.broadcasted_iota(I32, y_shape, 0)) + 2 * (y_lane // 64) - 1) * 2 + (
-        y_lane % 64
-    ) // 32
-    lane2 = lax.broadcasted_iota(I32, (16, 128), 1)
-    row2 = lax.broadcasted_iota(I32, (16, 128), 0)
-
-    def own(holder, j, out, at_slot):
-        w = tables[holder, j : j + 1, :]
-        w3, w4 = w.reshape(1, 1, 128), w.reshape(1, 1, 1, 128)
-        y_part = jnp.sum(jnp.where(y_id == w3, gathered[:, 4], 0.0), axis=0)
-        y_part = y_part + pltpu.roll(y_part, 64, 1)
-        y_part = y_part + pltpu.roll(y_part, 32, 1)
-        for t in range(2):
-            held = jnp.stack([gathered[:, t], gathered[:, 2 + t]], axis=1)
-            found = jnp.sum(jnp.where(piece_id == w4, held, 0.0), axis=(0, 1))
-            found = found + jnp.where(lane2 < 16 if t == 0 else lane2 >= 112, y_part, 0.0)
-            for side in range(2):
-                x_part = jnp.sum(
-                    jnp.where(x_id == w3, x_in[side, :, t], 0.0), axis=(0, 1)
-                ).reshape(1, 128)
-                found = found + jnp.where(row2 == (0 if side == 0 else 15), x_part, 0.0)
-            out[at_slot, :, 128 * t : 128 * t + 128] = found
-
-    for slot, holder in enumerate((3, 5)):
-        for j in range(2):
-            own(holder, j, sib_out, 2 * slot + j)
-    to_sib = remote(sib_out, sib_in, es_sem.at[0], er_sem.at[0], row_peers[0])
+    x_id = device_at(iota(x_shape, 0)) * 2 + iota(x_shape, 1)
+    y_shape = (n_y, SUB, 128)
+    y_lane = iota(y_shape, 2)
+    y_id = (device_at(iota(y_shape, 0)) + 2 * (y_lane // 32 % 2) - 1) * 2 + y_lane // 16 % 2
+    row8 = iota((SUB, 128), 0)
+    lane8 = iota((SUB, 128), 1)
+
+    def shell(holder, j):
+        w2 = want(holder, j)
+        w3, w4 = w2.reshape(1, 1, 128), w2.reshape(1, 1, 1, 128)
+        rows = jnp.sum(jnp.where(a_id == w4, late[:, 0:2], 0.0), axis=(0, 1))
+        edges = jnp.sum(jnp.where(b_id == w4, late[:, 2:4], 0.0), axis=0)
+        halves = [edges[n] + pltpu.roll(edges[n], 64, 1) for n in range(2)]
+        for side in range(2):
+            line = [
+                jnp.sum(jnp.where(x_id == w3, x_in[side, :, t], 0.0), axis=(0, 1)).reshape(1, 128)
+                for t in range(2)
+            ]
+            for t in range(2):
+                rows = rows + jnp.where(row8 == 4 * t + 3 * side, line[t], 0.0)
+            both_ends = jnp.where(lane8 < 32, line[0], pltpu.roll(line[1], 64, 1))
+            halves[side] = halves[side] + jnp.where(row8 == 7 * side, both_ends, 0.0)
+        found = jnp.where(y_id == w3, late[:, 4], 0.0)
+        for f in range(2):
+            part = jnp.sum(jnp.where(bulk[:, 8] == f, found, 0.0), axis=0)
+            part = part + pltpu.roll(part, 112, 1)
+            part = part + pltpu.roll(part, 96, 1)
+            spot = lane8 // 16 == 3 * f
+            for n in range(2):
+                turn = (48 * f + 64 * n) % 128
+                moved = pltpu.roll(part, turn, 1) if turn else part
+                halves[n] = halves[n] + jnp.where(spot, moved, 0.0)
+        return rows, halves
+
+    rows_of_shells = []
+    for h in (3, 2, 1, 0):
+        one, two = shell(holders[h], 0), shell(holders[h], 1)
+        shell_out[h, 0] = one[0]
+        shell_out[h, 1] = two[0]
+        for n in range(2):
+            shell_out[h, 2 + n] = jnp.where(lane8 < 64, one[1][n], pltpu.roll(two[1][n], 64, 1))
+        if h:
+            rows_of_shells.append(
+                remote(
+                    shell_out.at[h], shell_in.at[h - 1], es_sem.at[2 + h], er_sem.at[2 + h],
+                    row_peers[h - 1],
+                )
+            )
+    for copy in rows_of_bulk:
+        copy.wait_recv()
+    inner = bulk_out[0] + bulk_in[0] + bulk_in[1] + bulk_in[2]
+    for copy in rows_of_shells:
+        copy.wait_recv()
+    outer = shell_out[0] + shell_in[0] + shell_in[1] + shell_in[2]
     for j in range(2):
-        own(4, j, zp_out, j)
-        own(0, j, coarse, j)
-    to_sib.wait_recv()
-    for j in range(2):
-        zp_out[j] += sib_in[2 + j]
-    to_zpar = remote(zp_out, zp_in, es_sem.at[1], er_sem.at[1], row_peers[1])
-    for j in range(2):
-        coarse[j] += sib_in[j]
-    to_zpar.wait_recv()
-    for j in range(2):
-        coarse[j] += zp_in[j]
+        rows = outer[j]
+        turned = pltpu.roll(rows, 4, 0)
+        for n in range(2):
+            edges = outer[2 + n] if j == 0 else pltpu.roll(outer[2 + n], 64, 1)
+            for t in range(2):
+                line = rows if t == n else turned
+                found = jnp.where(row8 < 2 if n == 0 else row8 >= 6, line, inner[4 * j + 2 * t + n])
+                if t == 0:
+                    found = jnp.where(lane8 < 32, edges, found)
+                else:
+                    found = jnp.where(lane8 >= 96, pltpu.roll(edges, 64, 1), found)
+                coarse[j, SUB * n : SUB * n + SUB, 128 * t : 128 * t + 128] = found
     last = pltpu.make_async_copy(coarse, coarse_hbm, out_sem.at[1])
     last.start()
-    for copy in sent + wants + spread + [to_sib, to_zpar]:
+    for copy in sent + wants + early + spread + rows_of_bulk + rows_of_shells:
         copy.wait_send()
     store.wait()
     last.wait()
@@ -610,18 +697,18 @@
             pltpu.SMEM((2,), F32), pltpu.SMEM((2, 2), I32), pltpu.SMEM((2, 4), I32),
             pltpu.SMEM((1, 2, 2), I32), pltpu.SMEM((2,), I32),
         ]
-        + [vm(*big) for _ in range(14)]
+        + [vm(*big) for _ in range(15)]
         + [
-            vm(2, 2, LANES), vm(2, 2, CHUNKS, SUB, 128), vm(8, 64, 128), vm(512, 128), vm(256, 128),
+            vm(2, 2, LANES), vm(2, 2, CHUNKS, SUB, 128), vm(8, 64, 128), vm(512, 128), vm(128, 128),
             vm(2, 8, LANES), vm(2, 8, LANES),
             vm(2, 2 * CHUNKS + 1, SUB, 128), vm(2, 2 * CHUNKS + 1, SUB, 128),
             vm(2, 4, 128), vm(2, 2, 4, 128),
             pltpu.VMEM((6, SUB, 128), I32),
             vm(2, CHUNKS * SUB, 128),
-            vm(n_y, 5, 16, 128), vm(2, 2, 2, 128), vm(2, n_y, 2, 2, 128),
-            vm(4, 16, 256), vm(4, 16, 256), vm(2, 16, 256), vm(2, 16, 256), vm(2, 16, 256),
+            vm(n_y, 9, SUB, 128), vm(n_y, 5, SUB, 128), vm(2, 2, 2, 128), vm(2, n_y, 2, 2, 128),
+            vm(4, 8, SUB, 128), vm(3, 8, SUB, 128), vm(4, 4, SUB, 128), vm(3, 4, SUB, 128), vm(2, 16, 256),
             dma(8), dma(2), dma(8), dma(8), dma(5), dma(5), dma(n_y - 1), dma(n_y - 1),
-            dma(2 * n_y), dma(2 * n_y), dma(2), dma(2),
+            dma(n_y - 1), dma(n_y - 1), dma(2 * n_y), dma(2 * n_y), dma(6), dma(6),
         ],
         compiler_params=pltpu.CompilerParams(
             collective_id=0, has_side_effects=True, vmem_limit_bytes=32 * 1024 * 1024

time: 51.4 us -> 47.9 us (0.932)
  Pallas kernels: 49.3 us -> 45.5 us
    pallas_call x1, Pallas kernels: 49.3 us -> 45.5 us  [body(): pl.pallas_call(kernel, out_shape=(jax.ShapeDtypeStruct(big, F32), jax.Sha...]
where the time goes in v3:
time: 47.9 us; the launch traced here: 47.4 us
  Pallas kernels  45.5 us (95%)
  local copies, waits for them, and re-layouts  1.32 us (3%)
  between operations  0.64 us (1%)
    pallas_call x1, Pallas kernels, body(): pl.pallas_call(kernel, out_shape=(jax.ShapeDtypeStruct(big, F32), jax.Sha...  45.5 us
    unnamed x2, local copies, waits for them, and re-layouts  1.32 us

profile of v3, /device:TPU:7, one launch (start us, length us, event | category | flops | bytes accessed | tf_op | source)
XLA Modules:
  0.0 47.4 jit_solution(1558220590799145943)
XLA Ops:
  0.6 45.5 %shard_map.95 = (f32[2,4,8,1024]{3,2,1,0:T(8,128)S(1)}, f32[2,16,256]{2,1,0:T(8,128)S(1)}) custom-call(f32[2,4,8,1024]{3,2,1,0:T(8,128)} %bitcast.5, f32[2,4,8,1024]{3,2,1,0:T(8,128)} %bitcast.6, f32[2,4,8,1024]{3,2,1,0:T(8,128)} %bitcast.7, f32[2]{0:T(128)} %brink_hbm.1, s32[2,2]{1,0:T(2,128)} %ds_hbm.1, s32[2,4]{1,0:T(2,128)} %snt_hbm.1, ...), custom_call_target="tpu_custom_call" | custom-call | tf_op jit(solution)/shard_map/pallas_call | solution.py:688
  46.1 0.7 %copy.12 = f32[2,32,1024]{2,1,0:T(8,128)} copy(f32[2,32,1024]{2,1,0:T(8,128)S(1)} %bitcast.4) | data formatting | bytes 524288
  46.8 0.6 %copy.13 = f32[2,16,256]{2,1,0:T(8,128)} copy(f32[2,16,256]{2,1,0:T(8,128)S(1)} %get-tuple-element.9) | data formatting | bytes 65536

commit v4 on v3

--- a/solution.py
+++ b/solution.py
@@ -232,8 +232,9 @@
     lax.fori_loop(0, CHUNKS, weights, 0)
     loads[2].wait()
 
-    def neighbour_sum(field, into):
-        def step(k, _):
+    def neighbour_sum(field, into, first=0, stride=1, count=CHUNKS):
+        def step(n, _):
+            k = first + stride * n
             for a in range(2):
                 _, nbs = beside(field, a, k)
                 total = src[a, k]
@@ -242,7 +243,7 @@
                 into[a, k] = total
             return 0
 
-        lax.fori_loop(0, CHUNKS, step, 0)
+        lax.fori_loop(0, count, step, 0)
 
     neighbour_sum(u0, g)
     fill(g, dg, 1)
@@ -254,7 +255,7 @@
     fcol = lax.broadcasted_iota(I32, (128, 128), 1)
     pool_face[...] = 0.125 * (frow // 32 * 16 + (frow % 32) // 2 == fcol).astype(F32)
 
-    def pooled_residual(field, sums, more):
+    def pooled_residual(field, sums):
         def step(k, _):
             for a in range(2):
                 at_row = pl.multiple_of(a * 32 + k * SUB, SUB)
@@ -269,7 +270,7 @@
         ]
         stacked = [jnp.concatenate(paired[4 * h : 4 * h + 4], axis=1) for h in range(2)]
         return jnp.dot(
-            jnp.concatenate(stacked + more, axis=0), pool[...],
+            jnp.concatenate(stacked, axis=0), pool[...],
             preferred_element_type=F32, precision=lax.Precision.HIGHEST,
         )
 
@@ -293,7 +294,7 @@
         neighbour_sum(u1, ga)
         lax.fori_loop(0, CHUNKS, inner_second, 0)
         neighbour_sum(u2, ga)
-        pooled = pooled_residual(u2, ga, [])
+        pooled = pooled_residual(u2, ga)
         for a in range(2):
             for t in range(2):
                 n = 4 * a + 2 * t
@@ -301,7 +302,7 @@
         sides = jnp.where(quarter1 % 2 == 0, minus[0].astype(F32), minus[1].astype(F32))
         bulk[my_y, 8] = jnp.broadcast_to(sides, (SUB, 128))
 
-    inner_pieces()
+    pl.when(zh == 0)(inner_pieces)
     pl.semaphore_wait(barrier, greeted)
     sent = []
     for peer in range(2):
@@ -329,6 +330,7 @@
         remote(tables.at[0], tables.at[3 + j], ts_sem.at[2 + j], tr_sem.at[2 + j], device)
         for j, device in enumerate(row_peers)
     ]
+    pl.when(zh == 1)(inner_pieces)
     early = [
         remote(bulk.at[my_y], bulk.at[my_y], bs_sem.at[o], br_sem.at[o], device)
         for o, device in enumerate(y_peers)
@@ -495,24 +497,25 @@
         return 0
 
     lax.fori_loop(0, CHUNKS, first_update, 0)
-    neighbour_sum(u1, g)
     u_turned = rotated(py1)
+    y_flow = [
+        [wye[a, direction] * pick(codes[a][direction], u_turned) for direction in range(2)]
+        for a in range(2)
+    ]
+    x_flow = [[wxe[side, a : a + 1, :] * pick(ds[a, side], px1[side]) for side in range(2)] for a in range(2)]
+
+    def second_update(chunks):
+        for k in chunks:
+            for a in range(2):
+                g[a, k, :, 0:128] += y_flow[a][0][k]
+                g[a, k, :, LAST:LANES] += pltpu.roll(y_flow[a][1][k], 96, 1)
+                u2[a, k] = (1.0 - OMEGA) * u1[a, k] + inv[a, k] * g[a, k]
+
+    neighbour_sum(u1, g, 0, CHUNKS - 1, 2)
     for a in range(2):
         for side in range(2):
-            add_x(g, a, side, wxe[side, a : a + 1, :] * pick(ds[a, side], px1[side]))
-        for direction in range(2):
-            add_y(g, a, direction, wye[a, direction] * pick(codes[a][direction], u_turned))
-
-    def second_update(k, _):
-        for a in range(2):
-            u2[a, k] = (1.0 - OMEGA) * u1[a, k] + inv[a, k] * g[a, k]
-        return 0
-
-    lax.fori_loop(0, CHUNKS, second_update, 0)
-    store = pltpu.make_async_copy(u2, out_hbm, out_sem.at[0])
-    store.start()
-    neighbour_sum(u2, g)
-
+            add_x(g, a, side, x_flow[a][side])
+    second_update((0, CHUNKS - 1))
     across = []
     for side in range(2):
         flows = [wxe[side, a : a + 1, :] * x_face(u2, side, a) for a in range(2)]
@@ -522,7 +525,27 @@
                 total = total + jnp.where(ds[a, side] == s, flows[a], 0.0)
             across.append(total)
     across = jnp.concatenate(across, axis=0)
-    pooled = pooled_residual(u2, g, [across[:, 0:512], across[:, 512:1024]])
+    crossing = jnp.dot(
+        jnp.concatenate([across[:, 0:512], across[:, 512:1024]], axis=0), pool[...],
+        preferred_element_type=F32, precision=lax.Precision.HIGHEST,
+    )
+    for side in range(2):
+        for t in range(2):
+            x_out[side, t] = crossing[4 * t + 2 * side : 4 * t + 2 * side + 2, :]
+    spread = []
+    for side in range(2):
+        for o, device in enumerate(x_peers[side]):
+            n = side * n_y + o
+            spread.append(
+                Link(x_out.at[side], x_in.at[1 - side, my_y], xs_sem.at[n], xr_sem.at[n], device, side)
+            )
+    neighbour_sum(u1, g, 1, 1, CHUNKS - 2)
+    second_update(range(1, CHUNKS - 1))
+    store = pltpu.make_async_copy(u2, out_hbm, out_sem.at[0])
+    store.start()
+    neighbour_sum(u2, g)
+
+    pooled = pooled_residual(u2, g)
     lane2 = lax.broadcasted_iota(I32, (16, 128), 1)
     edges = jnp.zeros((16, 128), F32)
     for a in range(2):
@@ -533,10 +556,6 @@
             part = part if a == t else pltpu.roll(part, 64, 1)
             edges = jnp.where(lane2 // 32 == 2 * a + t, part, edges)
     late[my_y, 2:4] = edges.reshape(2, SUB, 128)
-    for side in range(2):
-        for t in range(2):
-            x_out[side, t] = pooled[64 + 4 * t + 2 * side : 66 + 4 * t + 2 * side, :]
-
     u_faces = own_faces(u2)
     for direction in range(2):
         total = jnp.zeros((CHUNKS, SUB, 128), F32)
@@ -559,16 +578,10 @@
     )
     late[my_y, 4] = jnp.where(lane2[0:8] < 64, faces[0:8], pltpu.roll(faces[8:16], 64, 1))
 
-    spread = [
+    spread += [
         remote(late.at[my_y], late.at[my_y], gs_sem.at[o], gr_sem.at[o], device)
         for o, device in enumerate(y_peers)
     ]
-    for side in range(2):
-        for o, device in enumerate(x_peers[side]):
-            n = side * n_y + o
-            spread.append(
-                Link(x_out.at[side], x_in.at[1 - side, my_y], xs_sem.at[n], xr_sem.at[n], device, side)
-            )
     for copy in wants + early:
         copy.wait_recv()
 
@@ -585,14 +598,19 @@
         return tables[holder, j : j + 1, :]
 
     holders = (0, 3, 4, 5)
-    for h in (2, 3, 1, 0):
+    for h, holder in ((2, 3), (3, 5), (1, 4), (0, 0)):
         held = bulk[:, 0:8].reshape(bulk_shape)
         for j in range(2):
-            w = want(holders[h], j).reshape(1, 1, 1, 1, 128)
+            w = want(holder, j).reshape(1, 1, 1, 1, 128)
             bulk_out[h, 4 * j : 4 * j + 4] = jnp.sum(jnp.where(bulk_id == w, held, 0.0), axis=(0, 1))
+        if h == 3:
+            to_core = remote(
+                bulk_out.at[pl.ds(2, 2)], bulk_in.at[pl.ds(0, 2)], es_sem.at[0], er_sem.at[0], row_peers[0]
+            )
+    to_core.wait_recv()
+    bulk_out[1] += bulk_in[1]
     rows_of_bulk = [
-        remote(bulk_out.at[1 + j], bulk_in.at[j], es_sem.at[j], er_sem.at[j], row_peers[j])
-        for j in (1, 2, 0)
+        to_core, remote(bulk_out.at[1], bulk_in.at[2], es_sem.at[1], er_sem.at[1], row_peers[1])
     ]
 
     for copy in spread:
@@ -650,9 +668,8 @@
                     row_peers[h - 1],
                 )
             )
-    for copy in rows_of_bulk:
-        copy.wait_recv()
-    inner = bulk_out[0] + bulk_in[0] + bulk_in[1] + bulk_in[2]
+    rows_of_bulk[1].wait_recv()
+    inner = bulk_out[0] + bulk_in[0] + bulk_in[2]
     for copy in rows_of_shells:
         copy.wait_recv()
     outer = shell_out[0] + shell_in[0] + shell_in[1] + shell_in[2]

time: 47.9 us -> 46.9 us (0.979)
  Pallas kernels: 45.5 us -> 44.4 us
    pallas_call x1, Pallas kernels: 45.5 us -> 44.4 us  [body(): pl.pallas_call(kernel, out_shape=(jax.ShapeDtypeStruct(big, F32), jax.Sha...]
where the time goes in v4:
time: 46.9 us; the launch traced here: 46.3 us
  Pallas kernels  44.4 us (95%)
  local copies, waits for them, and re-layouts  1.32 us (3%)
  between operations  0.64 us (1%)
    pallas_call x1, Pallas kernels, body(): pl.pallas_call(kernel, out_shape=(jax.ShapeDtypeStruct(big, F32), jax.Sha...  44.4 us
    unnamed x2, local copies, waits for them, and re-layouts  1.32 us

profile of v4, /device:TPU:7, one launch (start us, length us, event | category | flops | bytes accessed | tf_op | source)
XLA Modules:
  0.0 46.3 jit_solution(14024720206484922713)
XLA Ops:
  0.6 44.4 %shard_map.95 = (f32[2,4,8,1024]{3,2,1,0:T(8,128)S(1)}, f32[2,16,256]{2,1,0:T(8,128)S(1)}) custom-call(f32[2,4,8,1024]{3,2,1,0:T(8,128)} %bitcast.5, f32[2,4,8,1024]{3,2,1,0:T(8,128)} %bitcast.6, f32[2,4,8,1024]{3,2,1,0:T(8,128)} %bitcast.7, f32[2]{0:T(128)} %brink_hbm.1, s32[2,2]{1,0:T(2,128)} %ds_hbm.1, s32[2,4]{1,0:T(2,128)} %snt_hbm.1, ...), custom_call_target="tpu_custom_call" | custom-call | tf_op jit(solution)/shard_map/pallas_call | solution.py:705
  45.0 0.7 %copy.12 = f32[2,32,1024]{2,1,0:T(8,128)} copy(f32[2,32,1024]{2,1,0:T(8,128)S(1)} %bitcast.4) | data formatting | bytes 524288
  45.7 0.6 %copy.13 = f32[2,16,256]{2,1,0:T(8,128)} copy(f32[2,16,256]{2,1,0:T(8,128)S(1)} %get-tuple-element.9) | data formatting | bytes 65536

commit v5 on v4

--- a/solution.py
+++ b/solution.py
@@ -244,6 +244,35 @@
             return 0
 
         lax.fori_loop(0, count, step, 0)
+
+    outer_tiles = ((0, 0), (LANES - 256, 128))
+
+    def edge_sum(field, into):
+        def step(n, _):
+            k = 1 + n
+            for a in range(2):
+                for start, kept in outer_tiles:
+                    part = slice(start, start + 256)
+                    u = field[a, k, :, part]
+                    nm = field[zslot(a, 0), k, :, part]
+                    np_ = field[zslot(a, 1), k, :, part]
+                    before = field[a, k - 1, SUB - 1 : SUB, part]
+                    after = field[a, k + 1, 0:1, part]
+                    nbs = (
+                        jnp.where(row[:, 0:256] == 0, before, pltpu.roll(u, 1, 0)),
+                        jnp.where(row[:, 0:256] == SUB - 1, after, pltpu.roll(u, SUB - 1, 0)),
+                        pltpu.roll(u, 32, 1),
+                        pltpu.roll(u, 224, 1),
+                        jnp.where(zpos[:, 0:256] == 0, pltpu.roll(nm, 225, 1), pltpu.roll(u, 1, 1)),
+                        jnp.where(zpos[:, 0:256] == 31, pltpu.roll(np_, 31, 1), pltpu.roll(u, 255, 1)),
+                    )
+                    total = src[a, k, :, part]
+                    for store, nb in zip((wxm, wxp, wym, wyp, wzm, wzp), nbs):
+                        total = total + store[a, k, :, part] * nb
+                    into[a, k, :, start + kept : start + kept + 128] = total[:, kept : kept + 128]
+            return 0
+
+        lax.fori_loop(0, CHUNKS - 2, step, 0)
 
     neighbour_sum(u0, g)
     fill(g, dg, 1)
@@ -489,14 +518,15 @@
         gy = gy + jnp.where(rows3 == r, (w * values[0]).reshape(1, 1, 128), 0.0)
     py1 = (1.0 - OMEGA) * py + OMEGA * gy / dy
 
-    def first_update(k, _):
+    whole = slice(0, LANES)
+    parts = [(k, whole) for k in (0, CHUNKS - 1)]
+    parts += [(k, part) for k in range(1, CHUNKS - 1) for part in (slice(0, 128), slice(LAST, LANES))]
+    for k, part in parts:
         for a in range(2):
-            i = OMEGA / dg[a, k]
-            inv[a, k] = i
-            u1[a, k] = (1.0 - OMEGA) * u0[a, k] + i * g[a, k]
-        return 0
-
-    lax.fori_loop(0, CHUNKS, first_update, 0)
+            i = OMEGA / dg[a, k, :, part]
+            inv[a, k, :, part] = i
+            u1[a, k, :, part] = (1.0 - OMEGA) * u0[a, k, :, part] + i * g[a, k, :, part]
+
     u_turned = rotated(py1)
     y_flow = [
         [wye[a, direction] * pick(codes[a][direction], u_turned) for direction in range(2)]
@@ -504,18 +534,20 @@
     ]
     x_flow = [[wxe[side, a : a + 1, :] * pick(ds[a, side], px1[side]) for side in range(2)] for a in range(2)]
 
-    def second_update(chunks):
-        for k in chunks:
+    def second_update(chosen):
+        for k, part in chosen:
             for a in range(2):
-                g[a, k, :, 0:128] += y_flow[a][0][k]
-                g[a, k, :, LAST:LANES] += pltpu.roll(y_flow[a][1][k], 96, 1)
-                u2[a, k] = (1.0 - OMEGA) * u1[a, k] + inv[a, k] * g[a, k]
+                if part.start == 0:
+                    g[a, k, :, 0:128] += y_flow[a][0][k]
+                if part.stop == LANES:
+                    g[a, k, :, LAST:LANES] += pltpu.roll(y_flow[a][1][k], 96, 1)
+                u2[a, k, :, part] = (1.0 - OMEGA) * u1[a, k, :, part] + inv[a, k, :, part] * g[a, k, :, part]
 
     neighbour_sum(u1, g, 0, CHUNKS - 1, 2)
     for a in range(2):
         for side in range(2):
             add_x(g, a, side, x_flow[a][side])
-    second_update((0, CHUNKS - 1))
+    second_update(parts[0:2])
     across = []
     for side in range(2):
         flows = [wxe[side, a : a + 1, :] * x_face(u2, side, a) for a in range(2)]
@@ -539,11 +571,12 @@
             spread.append(
                 Link(x_out.at[side], x_in.at[1 - side, my_y], xs_sem.at[n], xr_sem.at[n], device, side)
             )
-    neighbour_sum(u1, g, 1, 1, CHUNKS - 2)
-    second_update(range(1, CHUNKS - 1))
+    edge_sum(u1, g)
+    second_update(parts[2:])
     store = pltpu.make_async_copy(u2, out_hbm, out_sem.at[0])
     store.start()
-    neighbour_sum(u2, g)
+    neighbour_sum(u2, g, 0, CHUNKS - 1, 2)
+    edge_sum(u2, g)
 
     pooled = pooled_residual(u2, g)
     lane2 = lax.broadcasted_iota(I32, (16, 128), 1)

time: 46.9 us -> 46.7 us (level)
  no operation moved by 1% of the time
where the time goes in v5:
time: 46.7 us; the launch traced here: 46.1 us
  Pallas kernels  44.2 us (95%)
  local copies, waits for them, and re-layouts  1.32 us (3%)
  between operations  0.64 us (1%)
    pallas_call x1, Pallas kernels, body(): pl.pallas_call(kernel, out_shape=(jax.ShapeDtypeStruct(big, F32), jax.Sha...  44.2 us
    unnamed x2, local copies, waits for them, and re-layouts  1.32 us

profile of v5, /device:TPU:7, one launch (start us, length us, event | category | flops | bytes accessed | tf_op | source)
XLA Modules:
  0.0 46.1 jit_solution(3027305663973878078)
XLA Ops:
  0.6 44.2 %shard_map.95 = (f32[2,4,8,1024]{3,2,1,0:T(8,128)S(1)}, f32[2,16,256]{2,1,0:T(8,128)S(1)}) custom-call(f32[2,4,8,1024]{3,2,1,0:T(8,128)} %bitcast.5, f32[2,4,8,1024]{3,2,1,0:T(8,128)} %bitcast.6, f32[2,4,8,1024]{3,2,1,0:T(8,128)} %bitcast.7, f32[2]{0:T(128)} %brink_hbm.1, s32[2,2]{1,0:T(2,128)} %ds_hbm.1, s32[2,4]{1,0:T(2,128)} %snt_hbm.1, ...), custom_call_target="tpu_custom_call" | custom-call | tf_op jit(solution)/shard_map/pallas_call | solution.py:738
  44.8 0.7 %copy.12 = f32[2,32,1024]{2,1,0:T(8,128)} copy(f32[2,32,1024]{2,1,0:T(8,128)S(1)} %bitcast.4) | data formatting | bytes 524288
  45.5 0.6 %copy.13 = f32[2,16,256]{2,1,0:T(8,128)} copy(f32[2,16,256]{2,1,0:T(8,128)S(1)} %get-tuple-element.9) | data formatting | bytes 65536

commit v6 on v5

--- a/solution.py
+++ b/solution.py
@@ -208,25 +208,30 @@
         zp = jnp.where(zpos == 31, pltpu.roll(np_, 31, 1), pltpu.roll(u, LANES - 1, 1))
         return u, (um, up, ym, yp, zm, zp)
 
-    def weights(k, _):
-        for a in range(2):
-            kk, nbs = beside(perm, a, k)
-            has_zm = snt[a, 2] >= 0
-            has_zp = snt[a, 3] >= 0
-            keep = (
-                jnp.logical_not((row == 0) & (k == 0)),
-                jnp.logical_not((row == SUB - 1) & (k == CHUNKS - 1)),
-                lane >= 32,
-                lane < LANES - 32,
-                jnp.logical_or(zpos != 0, has_zm),
-                jnp.logical_or(zpos != 31, has_zp),
-            )
-            total = jnp.full((SUB, LANES), brink[a], F32)
-            for store, nb, mask in zip((wxm, wxp, wym, wyp, wzm, wzp), nbs, keep):
-                w = jnp.where(mask, harmonic(kk, nb), 0.0)
-                store[a, k] = w
-                total = total + w
-            dg[a, k] = total
+    def weights(n, _):
+        k = CHUNKS - 1 - n
+        for a in range(2):
+            kk = perm[a, k]
+            before = perm[a, jnp.maximum(k - 1, 0), SUB - 1 : SUB, :]
+            um = jnp.where(row == 0, before, pltpu.roll(kk, 1, 0))
+            ym = pltpu.roll(kk, 32, 1)
+            nm = perm[zslot(a, 0), k]
+            zm = jnp.where(zpos == 0, pltpu.roll(nm, LANES - 31, 1), pltpu.roll(kk, 1, 1))
+            first = (row == 0) & (k == 0)
+            wxm[a, k] = jnp.where(first, 0.0, harmonic(kk, um))
+            wym[a, k] = jnp.where(lane >= 32, harmonic(kk, ym), 0.0)
+            wzm[a, k] = jnp.where((zpos != 0) | (snt[a, 2] >= 0), harmonic(kk, zm), 0.0)
+        for a in range(2):
+            after = wxm[a, jnp.minimum(k + 1, CHUNKS - 1), 0:1, :]
+            after = jnp.where(k == CHUNKS - 1, 0.0, after)
+            xp = jnp.where(row == SUB - 1, after, pltpu.roll(wxm[a, k], SUB - 1, 0))
+            yp = pltpu.roll(wym[a, k], LANES - 32, 1)
+            across_z = jnp.where(snt[a, 3] >= 0, pltpu.roll(wzm[zslot(a, 1), k], 31, 1), 0.0)
+            zp = jnp.where(zpos == 31, across_z, pltpu.roll(wzm[a, k], LANES - 1, 1))
+            wxp[a, k] = xp
+            wyp[a, k] = yp
+            wzp[a, k] = zp
+            dg[a, k] = brink[a] + wxm[a, k] + xp + wym[a, k] + yp + wzm[a, k] + zp
         return 0
 
     lax.fori_loop(0, CHUNKS, weights, 0)
@@ -279,10 +284,19 @@
 
     prow = lax.broadcasted_iota(I32, (512, 128), 0)
     pcol = lax.broadcasted_iota(I32, (512, 128), 1)
-    pool[...] = 0.125 * ((prow // 64) * 16 + (prow % 32) // 2 == pcol).astype(F32)
+    pool[...] = (0.125 * ((prow // 64) * 16 + (prow % 32) // 2 == pcol).astype(F32)).astype(jnp.bfloat16)
     frow = lax.broadcasted_iota(I32, (128, 128), 0)
     fcol = lax.broadcasted_iota(I32, (128, 128), 1)
-    pool_face[...] = 0.125 * (frow // 32 * 16 + (frow % 32) // 2 == fcol).astype(F32)
+    pool_face[...] = (0.125 * (frow // 32 * 16 + (frow % 32) // 2 == fcol).astype(F32)).astype(jnp.bfloat16)
+
+    def exact_dot(x, matrix):
+        high = x.astype(jnp.bfloat16).astype(F32)
+        rest = x - high
+        middle = rest.astype(jnp.bfloat16).astype(F32)
+        parts = jnp.concatenate([high, middle, rest - middle, jnp.zeros_like(x)], axis=0)
+        out = jnp.dot(parts.astype(jnp.bfloat16), matrix, preferred_element_type=F32)
+        n = x.shape[0]
+        return out[0:n] + out[n : 2 * n] + out[2 * n : 3 * n]
 
     def pooled_residual(field, sums):
         def step(k, _):
@@ -298,10 +312,7 @@
             res[t, pl.ds(0, 32, stride=2), :] + res[t, pl.ds(1, 32, stride=2), :] for t in range(8)
         ]
         stacked = [jnp.concatenate(paired[4 * h : 4 * h + 4], axis=1) for h in range(2)]
-        return jnp.dot(
-            jnp.concatenate(stacked, axis=0), pool[...],
-            preferred_element_type=F32, precision=lax.Precision.HIGHEST,
-        )
+        return exact_dot(jnp.concatenate(stacked, axis=0), pool[...])
 
     def piece_of(pooled, a, t):
         return pooled[32 * t + 16 * a : 32 * t + 16 * a + 16, :]
@@ -557,10 +568,7 @@
                 total = total + jnp.where(ds[a, side] == s, flows[a], 0.0)
             across.append(total)
     across = jnp.concatenate(across, axis=0)
-    crossing = jnp.dot(
-        jnp.concatenate([across[:, 0:512], across[:, 512:1024]], axis=0), pool[...],
-        preferred_element_type=F32, precision=lax.Precision.HIGHEST,
-    )
+    crossing = exact_dot(jnp.concatenate([across[:, 0:512], across[:, 512:1024]], axis=0), pool[...])
     for side in range(2):
         for t in range(2):
             x_out[side, t] = crossing[4 * t + 2 * side : 4 * t + 2 * side + 2, :]
@@ -605,10 +613,7 @@
     halves = [
         face_sum[direction, pl.ds(first, 16, stride=2), :] for direction in range(2) for first in range(2)
     ]
-    faces = jnp.dot(
-        halves[0] + halves[1] + halves[2] + halves[3], pool_face[...],
-        preferred_element_type=F32, precision=lax.Precision.HIGHEST,
-    )
+    faces = exact_dot(halves[0] + halves[1] + halves[2] + halves[3], pool_face[...])
     late[my_y, 4] = jnp.where(lane2[0:8] < 64, faces[0:8], pltpu.roll(faces[8:16], 64, 1))
 
     spread += [
@@ -749,7 +754,8 @@
         ]
         + [vm(*big) for _ in range(15)]
         + [
-            vm(2, 2, LANES), vm(2, 2, CHUNKS, SUB, 128), vm(8, 64, 128), vm(512, 128), vm(128, 128),
+            vm(2, 2, LANES), vm(2, 2, CHUNKS, SUB, 128), vm(8, 64, 128),
+            pltpu.VMEM((512, 128), jnp.bfloat16), pltpu.VMEM((128, 128), jnp.bfloat16),
             vm(2, 8, LANES), vm(2, 8, LANES),
             vm(2, 2 * CHUNKS + 1, SUB, 128), vm(2, 2 * CHUNKS + 1, SUB, 128),
             vm(2, 4, 128), vm(2, 2, 4, 128),

time: 46.7 us -> 46.6 us (level)
  no operation moved by 1% of the time
where the time goes in v6:
time: 46.6 us; the launch traced here: 46 us
  Pallas kernels  44.1 us (95%)
  local copies, waits for them, and re-layouts  1.32 us (3%)
  between operations  0.64 us (1%)
    pallas_call x1, Pallas kernels, body(): pl.pallas_call(kernel, out_shape=(jax.ShapeDtypeStruct(big, F32), jax.Sha...  44.1 us
    unnamed x2, local copies, waits for them, and re-layouts  1.32 us

profile of v6, /device:TPU:7, one launch (start us, length us, event | category | flops | bytes accessed | tf_op | source)
XLA Modules:
  0.0 46.0 jit_solution(11556220177906727816)
XLA Ops:
  0.6 44.1 %shard_map.95 = (f32[2,4,8,1024]{3,2,1,0:T(8,128)S(1)}, f32[2,16,256]{2,1,0:T(8,128)S(1)}) custom-call(f32[2,4,8,1024]{3,2,1,0:T(8,128)} %bitcast.5, f32[2,4,8,1024]{3,2,1,0:T(8,128)} %bitcast.6, f32[2,4,8,1024]{3,2,1,0:T(8,128)} %bitcast.7, f32[2]{0:T(128)} %brink_hbm.1, s32[2,2]{1,0:T(2,128)} %ds_hbm.1, s32[2,4]{1,0:T(2,128)} %snt_hbm.1, ...), custom_call_target="tpu_custom_call" | custom-call | tf_op jit(solution)/shard_map/pallas_call | solution.py:743
  44.7 0.7 %copy.12 = f32[2,32,1024]{2,1,0:T(8,128)} copy(f32[2,32,1024]{2,1,0:T(8,128)S(1)} %bitcast.4) | data formatting | bytes 524288
  45.4 0.6 %copy.13 = f32[2,16,256]{2,1,0:T(8,128)} copy(f32[2,16,256]{2,1,0:T(8,128)S(1)} %get-tuple-element.9) | data formatting | bytes 65536

commit v7 on v5

--- a/solution.py
+++ b/solution.py
@@ -44,9 +44,10 @@
     row_peers = [
         at(depth, my_y, zh, 1 - core), at(depth, my_y, 1 - zh, core), at(depth, my_y, 1 - zh, 1 - core)
     ]
-    y_peers = [at(depth, lax.rem(my_y + o, n_y), zh, core) for o in range(1, n_y)]
+    offsets = sorted(range(n_y), key=lambda o: -min(o, n_y - o))
+    y_peers = [at(depth, lax.rem(my_y + o, n_y), zh, core) for o in offsets if o]
     x_peers = [
-        [at(deeper[side], lax.rem(my_y + o, n_y), zh, core) for o in range(n_y)] for side in range(2)
+        [at(deeper[side], lax.rem(my_y + o, n_y), zh, core) for o in offsets] for side in range(2)
     ]
     i_peers = [(depth, m) for m in beside_me]
     d_peers = [(d, me) for d in deeper]

time: 46.7 us -> 46 us (0.985)
  Pallas kernels: 44.2 us -> 43.5 us
    pallas_call x1, Pallas kernels: 44.2 us -> 43.5 us  [body(): pl.pallas_call(kernel, out_shape=(jax.ShapeDtypeStruct(big, F32), jax.Sha...]
where the time goes in v7:
time: 46 us; the launch traced here: 45.5 us
  Pallas kernels  43.5 us (95%)
  local copies, waits for them, and re-layouts  1.32 us (3%)
  between operations  0.64 us (1%)
    pallas_call x1, Pallas kernels, body(): pl.pallas_call(kernel, out_shape=(jax.ShapeDtypeStruct(big, F32), jax.Sha...  43.5 us
    unnamed x2, local copies, waits for them, and re-layouts  1.32 us

profile of v7, /device:TPU:7, one launch (start us, length us, event | category | flops | bytes accessed | tf_op | source)
XLA Modules:
  0.0 45.5 jit_solution(15736913955546833389)
XLA Ops:
  0.6 43.5 %shard_map.95 = (f32[2,4,8,1024]{3,2,1,0:T(8,128)S(1)}, f32[2,16,256]{2,1,0:T(8,128)S(1)}) custom-call(f32[2,4,8,1024]{3,2,1,0:T(8,128)} %bitcast.5, f32[2,4,8,1024]{3,2,1,0:T(8,128)} %bitcast.6, f32[2,4,8,1024]{3,2,1,0:T(8,128)} %bitcast.7, f32[2]{0:T(128)} %brink_hbm.1, s32[2,2]{1,0:T(2,128)} %ds_hbm.1, s32[2,4]{1,0:T(2,128)} %snt_hbm.1, ...), custom_call_target="tpu_custom_call" | custom-call | tf_op jit(solution)/shard_map/pallas_call | solution.py:739
  44.2 0.7 %copy.12 = f32[2,32,1024]{2,1,0:T(8,128)} copy(f32[2,32,1024]{2,1,0:T(8,128)S(1)} %bitcast.4) | data formatting | bytes 524288
  44.9 0.6 %copy.13 = f32[2,16,256]{2,1,0:T(8,128)} copy(f32[2,16,256]{2,1,0:T(8,128)S(1)} %get-tuple-element.9) | data formatting | bytes 65536
